TPU v7x, 32 devices: a whole 2x2x4 slice. The times are simulated.
32 devices in a mesh: fsdp: 2 (over y), ctx: 4 (over x, core), tp: 4 (over z).
Axes of the slice: x: 2, y: 2, z: 4, core: 2. Of those that a mesh axis runs over, the one named last changes fastest.
Arguments:
- hidden_in: bfloat16 [4, 1024, 2048], P('fsdp', 'ctx'), may hold values from -6 to 6
- lengths: int32 [4], P('fsdp'), may hold values from 256 to 1024, as said below
- routes: int32 [4, 1024, 6], P('fsdp', 'ctx'), may hold values from 0 to 15, all different within a row; in each aligned block of 256 rows (0 to 255, 256 to 511, ..., all dimensions but the last counted through in order) at most 128 rows name the same one
- gate_weights: float32 [4, 1024, 6], P('fsdp', 'ctx'), may hold values from 0.1 to 0.5
- cotangent: bfloat16 [4, 1024, 2048], P('fsdp', 'ctx'), may hold values from -6 to 6
- attn_gain: bfloat16 [2048], P(('fsdp', 'ctx')), may hold values from 0.5 to 1.5
- query_weight: bfloat16 [2048, 3072], P(('fsdp', 'ctx'), 'tp'), may hold values from -0.125 to 0.125
- latent_down: bfloat16 [2048, 576], P(('fsdp', 'ctx')), may hold values from -0.125 to 0.125
- latent_gain: bfloat16 [512], P(('fsdp', 'ctx')), may hold values from 0.5 to 1.5
- latent_up: bfloat16 [512, 4096], P(('fsdp', 'ctx'), 'tp'), may hold values from -0.25 to 0.25
- output_weight: bfloat16 [2048, 2048], P('tp', ('fsdp', 'ctx')), may hold values from -0.375 to 0.375
- ffn_gain: bfloat16 [2048], P(('fsdp', 'ctx')), may hold values from 0.5 to 1.5
- shared_gate_up: bfloat16 [2048, 2, 2816], P(('fsdp', 'ctx'), None, 'tp'), may hold values from -0.125 to 0.125
- shared_down: bfloat16 [2816, 2048], P('tp', ('fsdp', 'ctx')), may hold values from -0.109375 to 0.109375
- expert_gate_up: bfloat16 [2048, 16, 2, 1408], P(('fsdp', 'ctx'), None, None, 'tp'), may hold values from -0.125 to 0.125
- expert_down: bfloat16 [2048, 16, 1408], P(('fsdp', 'ctx'), None, 'tp'), may hold values from -0.15625 to 0.15625
Outputs:
- block_out: bfloat16 [4, 1024, 2048], P('fsdp', 'ctx')
- input_grad: float32 [4, 1024, 2048], P('fsdp', 'ctx')
- attn_gain_grad: float32 [2048], P(('fsdp', 'ctx'))
- query_grad: float32 [2048, 3072], P(('fsdp', 'ctx'), 'tp')
- latent_down_grad: float32 [2048, 576], P(('fsdp', 'ctx'))
- latent_gain_grad: float32 [512], P(('fsdp', 'ctx'))
- latent_up_grad: float32 [512, 4096], P(('fsdp', 'ctx'), 'tp')
- output_grad: float32 [2048, 2048], P('tp', ('fsdp', 'ctx'))
- ffn_gain_grad: float32 [2048], P(('fsdp', 'ctx'))
- shared_gate_up_grad: float32 [2048, 2, 2816], P(('fsdp', 'ctx'), None, 'tp')
- shared_down_grad: float32 [2816, 2048], P('tp', ('fsdp', 'ctx'))
- expert_gate_up_grad: float32 [2048, 16, 2, 1408], P(('fsdp', 'ctx'), None, None, 'tp')
- expert_down_grad: float32 [2048, 16, 1408], P(('fsdp', 'ctx'), None, 'tp')
Inputs may be any that keep to these rules, and one draw needn't show every extreme that they name: `lengths`: in each group of 2 consecutive sequences, one has length 1024. `routes`: A position's 6 experts differ. In each sequence's aligned block of 256 positions no expert is named more than 128 times, and in some block one is named exactly 128 times.
All inputs are finite; a program needn't handle non-finite values.
Results may differ from a plain program's by a relative error of at most 0.024.
Values may be sent and summed in bfloat16 or wider, within the bound.
A program may use at most 512 MiB of HBM per device.

v0:
```python
import jax
import jax.numpy as jnp
from jax import lax
from jax.sharding import PartitionSpec as P

NOPE = 128
ROPE = 64
VDIM = 128
RANK = 512
TOP = 6
EXPERTS = 16


EPS = 1e-06


def rms_scale(values):
    return lax.rsqrt(jnp.mean(values * values, axis=-1, keepdims=True) + EPS)


def rotate(values, cosine, sine):
    half = values.shape[-1] // 2
    first = values[..., :half]
    second = values[..., half:]
    return jnp.concatenate([first * cosine - second * sine, first * sine + second * cosine], -1)


def rotate_back(grads, cosine, sine):
    half = grads.shape[-1] // 2
    first = grads[..., :half]
    second = grads[..., half:]
    return jnp.concatenate([first * cosine + second * sine, second * cosine - first * sine], -1)


def norm_back(values, scale, gain, grads):
    weighted = gain * grads
    return scale * weighted - values * (scale * scale * scale) * jnp.mean(
        weighted * values, axis=-1, keepdims=True
    )


def silu_parts(pre):
    sigma = jax.nn.sigmoid(pre)
    return (pre * sigma, sigma * (1.0 + pre * (1.0 - sigma)))


def expert_math(inputs, d_outs, gate_up, down, pieces):
    experts_here, slot_count, feature_count = inputs.shape
    unit_count = gate_up.shape[-1]
    piece_width = unit_count // pieces
    gate_up_pre = jnp.einsum("ecd,degf->ecgf", inputs, gate_up, preferred_element_type=jnp.float32)
    activated, slope = silu_parts(gate_up_pre[:, :, 0])
    hidden = (activated * gate_up_pre[:, :, 1]).astype(jnp.bfloat16)
    out_parts = jnp.einsum(
        "ecqf,deqf->ecqd",
        hidden.reshape(experts_here, slot_count, pieces, piece_width),
        down.reshape(feature_count, experts_here, pieces, piece_width),
        preferred_element_type=jnp.float32,
    ).astype(jnp.bfloat16)
    d_hidden = jnp.einsum("ecd,def->ecf", d_outs, down, preferred_element_type=jnp.float32)
    d_gate_up = jnp.stack(
        [d_hidden * gate_up_pre[:, :, 1] * slope, d_hidden * activated], 2
    ).astype(jnp.bfloat16)
    in_parts = jnp.einsum(
        "ecgqf,degqf->ecqd",
        d_gate_up.reshape(experts_here, slot_count, 2, pieces, piece_width),
        gate_up.reshape(feature_count, experts_here, 2, pieces, piece_width),
        preferred_element_type=jnp.float32,
    ).astype(jnp.bfloat16)
    return (out_parts, in_parts, hidden, d_gate_up)


def local(
    hidden_in,
    lengths,
    routes,
    gate_weights,
    cotangent,
    attn_gain,
    query_weight,
    latent_down,
    latent_gain,
    latent_up,
    output_weight,
    ffn_gain,
    shared_gate_up,
    shared_down,
    expert_gate_up,
    expert_down,
):
    seq_dev, block, width = hidden_in.shape
    (
        gain_one,
        query_full,
        down_full,
        lat_gain,
        up_full,
        out_full,
        gain_two,
        shared_full,
        sdown_full,
    ) = (
        lax.all_gather(attn_gain, ("fsdp", "ctx"), axis=0, tiled=True),
        lax.all_gather(query_weight, ("fsdp", "ctx"), axis=0, tiled=True),
        lax.all_gather(latent_down, ("fsdp", "ctx"), axis=0, tiled=True),
        lax.all_gather(latent_gain, ("fsdp", "ctx"), axis=0, tiled=True),
        lax.all_gather(latent_up, ("fsdp", "ctx"), axis=0, tiled=True),
        lax.all_gather(output_weight, ("fsdp", "ctx"), axis=1, tiled=True),
        lax.all_gather(ffn_gain, ("fsdp", "ctx"), axis=0, tiled=True),
        lax.all_gather(shared_gate_up, ("fsdp", "ctx"), axis=0, tiled=True),
        lax.all_gather(shared_down, ("fsdp", "ctx"), axis=1, tiled=True),
    )
    gain_one = gain_one.astype(jnp.float32)
    lat_gain = lat_gain.astype(jnp.float32)
    gain_two = gain_two.astype(jnp.float32)
    head_dim = NOPE + ROPE
    heads_dev = query_full.shape[1] // head_dim
    total_len = block * lax.axis_size("ctx")
    positions = lax.axis_index("ctx") * block + jnp.arange(block, dtype=jnp.int32)
    inverse = 10000.0 ** (-jnp.arange(ROPE // 2, dtype=jnp.float32) / (ROPE // 2))
    angles = positions.astype(jnp.float32)[:, None] * inverse[None, :]
    cosine = jnp.cos(angles)
    sine = jnp.sin(angles)
    scale = float(head_dim) ** (-0.5)
    input_f = hidden_in.astype(jnp.float32)
    scale_one = rms_scale(input_f)
    low_one = (input_f * scale_one * gain_one).astype(jnp.bfloat16)
    query_pre = jnp.einsum(
        "sbd,dk->sbk", low_one, query_full, preferred_element_type=jnp.float32
    ).reshape(seq_dev, block, heads_dev, head_dim)
    queries = jnp.concatenate(
        [
            query_pre[..., :NOPE],
            rotate(query_pre[..., NOPE:], cosine[None, :, None], sine[None, :, None]),
        ],
        -1,
    ).astype(jnp.bfloat16)
    latent_pre = jnp.einsum("sbd,dk->sbk", low_one, down_full, preferred_element_type=jnp.float32)
    latent = latent_pre[..., :RANK]
    scale_lat = rms_scale(latent)
    lat_low = (latent * scale_lat * lat_gain).astype(jnp.bfloat16)
    rope_low = rotate(latent_pre[..., RANK:], cosine[None], sine[None]).astype(jnp.bfloat16)
    lat_keys, rope_keys = (
        lax.all_gather(lat_low, "ctx", axis=1, tiled=True),
        lax.all_gather(rope_low, "ctx", axis=1, tiled=True),
    )
    expanded = jnp.einsum(
        "sjr,rk->sjk", lat_keys, up_full, preferred_element_type=jnp.float32
    ).astype(jnp.bfloat16)
    expanded = expanded.reshape(seq_dev, total_len, heads_dev, NOPE + VDIM)
    key_nope = expanded[..., :NOPE]
    values = expanded[..., NOPE:]
    key_pos = jnp.arange(total_len, dtype=jnp.int32)
    keep = (key_pos[None, None, :] <= positions[None, :, None]) & (
        key_pos[None, None, :] < lengths[:, None, None]
    )
    keep = keep[:, None]
    raw = jnp.einsum(
        "sihd,sjhd->shij", queries[..., :NOPE], key_nope, preferred_element_type=jnp.float32
    )
    raw = raw + jnp.einsum(
        "sihe,sje->shij", queries[..., NOPE:], rope_keys, preferred_element_type=jnp.float32
    )
    masked = jnp.where(keep, raw * scale, -1e30)
    peak = jnp.max(masked, axis=-1, keepdims=True)
    expo = jnp.exp(masked - peak)
    totals = jnp.sum(expo, axis=-1, keepdims=True)
    probs = expo / totals
    log_total = peak + jnp.log(totals)
    attended = jnp.einsum(
        "shij,sjhd->sihd", probs.astype(jnp.bfloat16), values, preferred_element_type=jnp.float32
    )
    attended = attended.astype(jnp.bfloat16).reshape(seq_dev, block, heads_dev * VDIM)
    attn_part = jnp.einsum("sbk,kd->sbd", attended, out_full, preferred_element_type=jnp.float32)
    middle = input_f + lax.psum(attn_part, "tp")
    scale_two = rms_scale(middle)
    low_two = (middle * scale_two * gain_two).astype(jnp.bfloat16)
    shared_gu = jnp.einsum(
        "sbd,dgf->sbgf", low_two, shared_full, preferred_element_type=jnp.float32
    )
    shared_act, shared_slope = silu_parts(shared_gu[:, :, 0])
    shared_hidden = (shared_act * shared_gu[:, :, 1]).astype(jnp.bfloat16)
    shared_out = jnp.einsum(
        "sbf,fd->sbd", shared_hidden, sdown_full, preferred_element_type=jnp.float32
    )
    valid = (positions[None, :] < lengths[:, None]).astype(jnp.float32)
    grad_out = cotangent.astype(jnp.float32) * valid[:, :, None]
    tokens_dev = seq_dev * block
    capacity = seq_dev * (block // 2)
    flat_routes = routes.reshape(-1)
    onehot = (flat_routes[:, None] == jnp.arange(EXPERTS, dtype=jnp.int32)[None, :]).astype(
        jnp.int32
    )
    ranks = jnp.sum((jnp.cumsum(onehot, axis=0) - onehot) * onehot, axis=1)
    slots = flat_routes * capacity + ranks
    owners = (
        jnp.zeros((EXPERTS * capacity,), jnp.int32)
        .at[slots]
        .set(jnp.arange(tokens_dev * TOP, dtype=jnp.int32) // TOP)
    )
    filled = jnp.zeros((EXPERTS * capacity,), jnp.bfloat16).at[slots].set(1.0)
    slot_gates = (
        jnp.zeros((EXPERTS * capacity,), jnp.float32).at[slots].set(gate_weights.reshape(-1))
    )
    slot_inputs = (low_two.reshape(tokens_dev, width)[owners] * filled[:, None]).reshape(
        EXPERTS, capacity, width
    )
    d_slot_out = (
        (slot_gates[:, None] * grad_out.reshape(tokens_dev, width)[owners])
        .astype(jnp.bfloat16)
        .reshape(EXPERTS, capacity, width)
    )
    expert_width = expert_gate_up.shape[-1]
    rows_local = expert_gate_up.shape[0]
    fold_size = lax.axis_size("fsdp") * lax.axis_size("ctx")
    repeat_count = max(fold_size // EXPERTS, 1)
    piece_width = expert_width // repeat_count
    gu_columns = expert_gate_up.reshape(
        rows_local, EXPERTS, 2, repeat_count, piece_width
    ).transpose(0, 1, 3, 2, 4)
    gu_columns = gu_columns.reshape(rows_local, EXPERTS * repeat_count, 2, piece_width)
    down_columns = expert_down.reshape(rows_local, EXPERTS * repeat_count, piece_width)
    gu_owned, down_owned = (
        lax.all_to_all(gu_columns, ("fsdp", "ctx"), split_axis=1, concat_axis=0, tiled=True),
        lax.all_to_all(down_columns, ("fsdp", "ctx"), split_axis=1, concat_axis=0, tiled=True),
    )
    send_inputs = jnp.repeat(slot_inputs, repeat_count, axis=0)
    send_grads = jnp.repeat(d_slot_out, repeat_count, axis=0)
    recv_inputs, recv_grads = (
        lax.all_to_all(send_inputs, ("fsdp", "ctx"), split_axis=0, concat_axis=1, tiled=True),
        lax.all_to_all(send_grads, ("fsdp", "ctx"), split_axis=0, concat_axis=1, tiled=True),
    )
    out_parts, in_parts, owned_hidden, owned_d_gu = expert_math(
        recv_inputs, recv_grads, gu_owned, down_owned, 1
    )
    back_out, back_in = (
        lax.all_to_all(
            out_parts[:, :, 0], ("fsdp", "ctx"), split_axis=1, concat_axis=0, tiled=True
        ),
        lax.all_to_all(in_parts[:, :, 0], ("fsdp", "ctx"), split_axis=1, concat_axis=0, tiled=True),
    )
    slot_out = (
        back_out.astype(jnp.float32).reshape(EXPERTS, repeat_count, capacity, width).sum(axis=1)
    )
    d_slot_in = (
        back_in.astype(jnp.float32).reshape(EXPERTS, repeat_count, capacity, width).sum(axis=1)
    )
    owned_gu_grad = jnp.einsum(
        "ecd,ecgf->degf", recv_inputs, owned_d_gu, preferred_element_type=jnp.float32
    )
    owned_down_grad = jnp.einsum(
        "ecd,ecf->def", recv_grads, owned_hidden, preferred_element_type=jnp.float32
    )
    gu_home, down_home = (
        lax.all_to_all(
            owned_gu_grad.astype(jnp.bfloat16),
            ("fsdp", "ctx"),
            split_axis=0,
            concat_axis=1,
            tiled=True,
        ).astype(owned_gu_grad.dtype),
        lax.all_to_all(
            owned_down_grad.astype(jnp.bfloat16),
            ("fsdp", "ctx"),
            split_axis=0,
            concat_axis=1,
            tiled=True,
        ).astype(owned_down_grad.dtype),
    )
    gate_up_grad = gu_home.reshape(rows_local, EXPERTS, repeat_count, 2, piece_width).transpose(
        0, 1, 3, 2, 4
    )
    gate_up_grad = gate_up_grad.reshape(rows_local, EXPERTS, 2, expert_width)
    down_grad = down_home.reshape(rows_local, EXPERTS, expert_width)
    picked = slot_out.reshape(EXPERTS * capacity, width)[slots].reshape(tokens_dev, TOP, width)
    routed = jnp.sum(gate_weights.reshape(tokens_dev, TOP, 1) * picked, axis=1)
    moe_part = shared_out + routed.reshape(seq_dev, block, width)
    block_out = (middle + lax.psum(moe_part.astype(jnp.bfloat16), "tp").astype(jnp.float32)).astype(
        jnp.bfloat16
    )
    grad_low = grad_out.astype(jnp.bfloat16)
    d_shared_hidden = jnp.einsum(
        "sbd,fd->sbf", grad_low, sdown_full, preferred_element_type=jnp.float32
    )
    d_shared_gu = jnp.stack(
        [d_shared_hidden * shared_gu[:, :, 1] * shared_slope, d_shared_hidden * shared_act], 2
    ).astype(jnp.bfloat16)
    shared_down_g = jnp.einsum(
        "sbf,sbd->fd", shared_hidden, grad_low, preferred_element_type=jnp.float32
    )
    shared_gu_g = jnp.einsum(
        "sbd,sbgf->dgf", low_two, d_shared_gu, preferred_element_type=jnp.float32
    )
    d_shared_in = jnp.einsum(
        "sbgf,dgf->sbd", d_shared_gu, shared_full, preferred_element_type=jnp.float32
    )
    d_routed_in = (
        d_slot_in.reshape(EXPERTS * capacity, width)[slots]
        .reshape(tokens_dev, TOP, width)
        .sum(axis=1)
    )
    d_low_two = lax.psum(d_shared_in + d_routed_in.reshape(seq_dev, block, width), "tp")
    ffn_gain_g = jnp.sum(d_low_two * middle * scale_two, axis=(0, 1))
    d_middle = grad_out + norm_back(middle, scale_two, gain_two, d_low_two)
    d_branch = d_middle.astype(jnp.bfloat16)
    output_g = jnp.einsum("sbk,sbd->kd", attended, d_branch, preferred_element_type=jnp.float32)
    d_attended = jnp.einsum("sbd,kd->sbk", d_branch, out_full, preferred_element_type=jnp.float32)
    d_attended = d_attended.astype(jnp.bfloat16).reshape(seq_dev, block, heads_dev, VDIM)
    again_raw = jnp.einsum(
        "sihd,sjhd->shij", queries[..., :NOPE], key_nope, preferred_element_type=jnp.float32
    )
    again_raw = again_raw + jnp.einsum(
        "sihe,sje->shij", queries[..., NOPE:], rope_keys, preferred_element_type=jnp.float32
    )
    again_probs = jnp.exp(jnp.where(keep, again_raw * scale, -1e30) - log_total)
    d_probs = jnp.einsum("sihd,sjhd->shij", d_attended, values, preferred_element_type=jnp.float32)
    d_scores = again_probs * (d_probs - jnp.sum(again_probs * d_probs, axis=-1, keepdims=True))
    d_scores = d_scores.astype(jnp.bfloat16)
    d_query_nope = (
        jnp.einsum("shij,sjhd->sihd", d_scores, key_nope, preferred_element_type=jnp.float32)
        * scale
    )
    d_query_rope = (
        jnp.einsum("shij,sje->sihe", d_scores, rope_keys, preferred_element_type=jnp.float32)
        * scale
    )
    d_key_nope = (
        jnp.einsum(
            "shij,sihd->sjhd", d_scores, queries[..., :NOPE], preferred_element_type=jnp.float32
        )
        * scale
    )
    d_rope_part = (
        jnp.einsum(
            "shij,sihe->sje", d_scores, queries[..., NOPE:], preferred_element_type=jnp.float32
        )
        * scale
    )
    d_values = jnp.einsum(
        "shij,sihd->sjhd",
        again_probs.astype(jnp.bfloat16),
        d_attended,
        preferred_element_type=jnp.float32,
    )
    d_expanded = (
        jnp.concatenate([d_key_nope, d_values], -1)
        .astype(jnp.bfloat16)
        .reshape(seq_dev, total_len, heads_dev * (NOPE + VDIM))
    )
    latent_up_g = jnp.einsum(
        "sjr,sjk->rk", lat_keys, d_expanded, preferred_element_type=jnp.float32
    )
    d_lat_part = jnp.einsum("sjk,rk->sjr", d_expanded, up_full, preferred_element_type=jnp.float32)
    d_lat_ctx, d_rope_ctx = (
        lax.psum_scatter(
            d_lat_part.astype(jnp.bfloat16), "ctx", scatter_dimension=1, tiled=True
        ).astype(jnp.float32),
        lax.psum_scatter(
            d_rope_part.astype(jnp.bfloat16), "ctx", scatter_dimension=1, tiled=True
        ).astype(jnp.float32),
    )
    d_query_pre = jnp.concatenate(
        [d_query_nope, rotate_back(d_query_rope, cosine[None, :, None], sine[None, :, None])], -1
    )
    d_query_pre = d_query_pre.astype(jnp.bfloat16).reshape(seq_dev, block, heads_dev * head_dim)
    query_g = jnp.einsum("sbd,sbk->dk", low_one, d_query_pre, preferred_element_type=jnp.float32)
    d_query_in = jnp.einsum(
        "sbk,dk->sbd", d_query_pre, query_full, preferred_element_type=jnp.float32
    )
    d_lat_keys, d_rope_keys, d_query_in = (
        lax.psum(d_lat_ctx.astype(jnp.bfloat16), "tp").astype(jnp.float32),
        lax.psum(d_rope_ctx.astype(jnp.bfloat16), "tp").astype(jnp.float32),
        lax.psum(d_query_in.astype(jnp.bfloat16), "tp").astype(jnp.float32),
    )
    latent_gain_g = jnp.sum(d_lat_keys * latent * scale_lat, axis=(0, 1))
    d_latent = norm_back(latent, scale_lat, lat_gain, d_lat_keys)
    d_latent_pre = jnp.concatenate(
        [d_latent, rotate_back(d_rope_keys, cosine[None], sine[None])], -1
    ).astype(jnp.bfloat16)
    latent_down_g = jnp.einsum(
        "sbd,sbk->dk", low_one, d_latent_pre, preferred_element_type=jnp.float32
    )
    d_low_one = d_query_in + jnp.einsum(
        "sbk,dk->sbd", d_latent_pre, down_full, preferred_element_type=jnp.float32
    )
    attn_gain_g = jnp.sum(d_low_one * input_f * scale_one, axis=(0, 1))
    input_grad = d_middle + norm_back(input_f, scale_one, gain_one, d_low_one)
    (
        attn_gain_s,
        query_s,
        down_s,
        lat_gain_s,
        up_s,
        output_s,
        ffn_gain_s,
        shared_gu_s,
        shared_down_s,
    ) = (
        lax.psum_scatter(
            attn_gain_g.astype(jnp.bfloat16), ("fsdp", "ctx"), scatter_dimension=0, tiled=True
        ).astype(jnp.float32),
        lax.psum_scatter(
            query_g.astype(jnp.bfloat16), ("fsdp", "ctx"), scatter_dimension=0, tiled=True
        ).astype(jnp.float32),
        lax.psum_scatter(
            latent_down_g.astype(jnp.bfloat16), ("fsdp", "ctx"), scatter_dimension=0, tiled=True
        ).astype(jnp.float32),
        lax.psum_scatter(
            latent_gain_g.astype(jnp.bfloat16), ("fsdp", "ctx"), scatter_dimension=0, tiled=True
        ).astype(jnp.float32),
        lax.psum_scatter(
            latent_up_g.astype(jnp.bfloat16), ("fsdp", "ctx"), scatter_dimension=0, tiled=True
        ).astype(jnp.float32),
        lax.psum_scatter(
            output_g.astype(jnp.bfloat16), ("fsdp", "ctx"), scatter_dimension=1, tiled=True
        ).astype(jnp.float32),
        lax.psum_scatter(
            ffn_gain_g.astype(jnp.bfloat16), ("fsdp", "ctx"), scatter_dimension=0, tiled=True
        ).astype(jnp.float32),
        lax.psum_scatter(
            shared_gu_g.astype(jnp.bfloat16), ("fsdp", "ctx"), scatter_dimension=0, tiled=True
        ).astype(jnp.float32),
        lax.psum_scatter(
            shared_down_g.astype(jnp.bfloat16), ("fsdp", "ctx"), scatter_dimension=1, tiled=True
        ).astype(jnp.float32),
    )
    return (
        block_out,
        input_grad,
        attn_gain_s,
        query_s,
        down_s,
        lat_gain_s,
        up_s,
        output_s,
        ffn_gain_s,
        shared_gu_s,
        shared_down_s,
        gate_up_grad,
        down_grad,
    )


def solution(mesh):
    placed = (
        P("fsdp", "ctx", None),
        P("fsdp"),
        P("fsdp", "ctx", None),
        P("fsdp", "ctx", None),
        P("fsdp", "ctx", None),
        P(("fsdp", "ctx")),
        P(("fsdp", "ctx"), "tp"),
        P(("fsdp", "ctx"), None),
        P(("fsdp", "ctx")),
        P(("fsdp", "ctx"), "tp"),
        P("tp", ("fsdp", "ctx")),
        P(("fsdp", "ctx")),
        P(("fsdp", "ctx"), None, "tp"),
        P("tp", ("fsdp", "ctx")),
        P(("fsdp", "ctx"), None, None, "tp"),
        P(("fsdp", "ctx"), None, "tp"),
    )
    return jax.shard_map(
        local,
        mesh=mesh,
        in_specs=placed,
        out_specs=(
            P("fsdp", "ctx", None),
            P("fsdp", "ctx", None),
            P(("fsdp", "ctx")),
            P(("fsdp", "ctx"), "tp"),
            P(("fsdp", "ctx"), None),
            P(("fsdp", "ctx")),
            P(("fsdp", "ctx"), "tp"),
            P("tp", ("fsdp", "ctx")),
            P(("fsdp", "ctx")),
            P(("fsdp", "ctx"), None, "tp"),
            P("tp", ("fsdp", "ctx")),
            P(("fsdp", "ctx"), None, None, "tp"),
            P(("fsdp", "ctx"), None, "tp"),
        ),
        check_vma=False,
    )
```

profile of v0, /device:TPU:0, one launch (start us, length us, event | category | flops | bytes accessed | tf_op | source)
XLA Modules:
  0.0 2012.7 jit_solution(11636675808244221712)
XLA Ops:
  21.1 37.3 %all-to-all-done.2 = bf16[256,16,352]{0,2,1:T(8,128)(2,1)S(1)} async-done(((bf16[256,16,352]{0,2,1:T(8,128)(2,1)}), bf16[256,16,352]{0,2,1:T(8,128)(2,1)S(1)}, u32[]{:S(2)}, u32[]{:S(2)}) %all-to-all-start.2) | async-done | bytes 2883616 | tf_op jit(solution)/shard_map/all_to_all | solution.py:225
  68.8 77.5 %all-gather = bf16[8,1,256]{2,1,0:T(2,128)(2,1)S(1)} all-gather(bf16[1,1,256]{2,1,0:T(2,128)(2,1)S(1)} %reshape.537), channel_id=1, replica_groups=mesh['fsdp'=2,'ctx'=4,'tp'=4] {'fsdp','ctx'}, dimensions={0}, use_global_device_ids=true | all-gather | bytes 4608 | tf_op jit(solution)/shard_map/all_gather | solution.py:103
  147.8 12.2 all-reduce
  160.3 11.8 scatter_custom_fusion
  172.1 11.8 scatter_custom_fusion.2
  184.0 34.0 %gather_fusion.2 = f32[4096,2048]{1,0:T(8,128)} fusion(f32[512,2048]{1,0:T(8,128)} %bitcast.311, s32[4096]{0:T(1024)S(1)} %fusion.121), kind=kCustom, calls=%fused_computation.2 | custom fusion | bytes 67125248 | tf_op jit(solution)/shard_map/gather | solution.py:209
  224.0 17.6 multiply_convert_fusion
  241.7 5.7 all-to-all-start.4
  249.7 191.3 %all_gather.39 = bf16[2,1024,64]{1,2,0:T(8,128)(2,1)S(1)} all-gather(bf16[2,256,64]{1,2,0:T(8,128)(2,1)S(1)} %pad_maximum_fusion.12), channel_id=1, replica_groups=mesh['fsdp'=2,'ctx'=4,'tp'=4] {'ctx'}, dimensions={1}, use_global_device_ids=true | all-gather | bytes 327680 | tf_op jit(solution)/shard_map/all_gather | solution.py:145
  465.5 8.9 all-gather.1
  474.5 21.6 %scatter_custom_fusion.1 = bf16[4096]{0:T(1024)(128)(2,1)S(1)} fusion(s32[3072]{0:T(1024)S(1)} %bitcast.357, bf16[3072]{0:T(1024)(128)(2,1)S(1)} %broadcast.320, bf16[]{:T(256)} %constant.65.clone.1), kind=kCustom, calls=%fused_computation.207 | custom fusion | bytes 8194 | tf_op jit(solution)/shard_map/scatter | solution.py:201
  496.1 125.0 %all-reduce.10.cloned.1.call-done = f32[2,256,2048]{2,1,0:T(8,128)} async-done(((f32[2,256,2048]{2,1,0:T(8,128)}), f32[2,256,2048]{2,1,0:T(8,128)}) %all-reduce.10.cloned.1.call-update) | async-done | bytes 4194320 | tf_op jit(solution)/shard_map/psum | solution.py:175
  626.3 20.9 %gather_fusion = bf16[4096,2048]{1,0:T(8,128)(2,1)} fusion(bf16[512,2048]{1,0:T(8,128)(2,1)S(1)} %bitcast.312, s32[4096]{0:T(1024)S(1)} %fusion.121), kind=kCustom, calls=%fused_computation | custom fusion | bytes 33570816 | tf_op jit(solution)/shard_map/gather | solution.py:205
  647.2 14.0 broadcast_multiply_fusion
  661.3 5.7 all-to-all-start
  667.0 8.4 all-gather.20.cloned.1.call-start
  680.4 5.6 reshape.460
  686.0 8.5 copy.207
  694.5 9.8 all_to_all.85
  704.4 14.2 copy.154
  718.6 155.6 %all-to-all-done = bf16[16,256,2048]{2,1,0:T(8,128)(2,1)} async-done(((bf16[16,256,2048]{2,1,0:T(8,128)(2,1)}), bf16[16,256,2048]{2,1,0:T(8,128)(2,1)}, u32[]{:S(2)}, u32[]{:S(2)}) %all-to-all-start) | async-done | bytes 16777248 | tf_op jit(solution)/shard_map/all_to_all | solution.py:230
  874.1 14.2 copy.146
  888.3 19.9 fusion.146
  908.1 15.9 fusion.56
  924.0 20.3 %bitcast_convert_fusion = bf16[2,2048,2048]{2,1,0:T(8,128)(2,1)} fusion(bf16[2048,2,2,352]{0,3,2,1:T(8,128)(2,1)} %all_to_all.85, bf16[2,2048,1,352]{1,3,0,2:T(8,128)(2,1)} %get-tuple-element.29, bf16[2,2048,1,352]{1,3,0,2:T(8,128)(2,1)} %get-tuple-element.28), kind=kOutput, calls=%fused_computation.7 | convolution fusion | flops 11822432256 | bytes 28311552 | tf_op jit(solution)/shard_map/ecgqf,degqf->ecqd/dot_general | solution.py:64
  944.3 31.0 %copy.156 = bf16[2,2048,2048]{2,0,1:T(2,128)(2,1)} copy(bf16[2,2048,2048]{2,1,0:T(8,128)(2,1)} %bitcast_convert_fusion) | data formatting | bytes 33554432 | tf_op jit(solution)/shard_map/convert_element_type | solution.py:69
  975.3 5.9 all-to-all-start.5
  982.2 7.4 fusion.18
  989.6 107.2 %all-gather.22.cloned.1.call-done = bf16[704,2048]{1,0:T(8,128)(2,1)} async-done(((bf16[704,256]{1,0:T(8,128)(2,1)}), bf16[704,2048]{1,0:T(8,128)(2,1)}) %all-gather.22.cloned.1.call-update) | async-done | bytes 2883600 | tf_op jit(solution)/shard_map/all_gather | solution.py:111
  1096.8 6.4 fusion.110
  1103.2 73.5 %all-to-all-done.5 = bf16[2,2048,2048]{2,0,1:T(2,128)(2,1)} async-done(((bf16[2,2048,2048]{2,0,1:T(2,128)(2,1)}), bf16[2,2048,2048]{2,0,1:T(2,128)(2,1)}, u32[]{:S(2)}, u32[]{:S(2)}) %all-to-all-start.5) | async-done | bytes 16777248 | tf_op jit(solution)/shard_map/all_to_all | solution.py:240
  1176.7 19.6 copy.157
  1196.3 34.6 %gather_fusion.3 = f32[3072,2048]{1,0:T(8,128)} fusion(f32[4096,2048]{1,0:T(8,128)} %bitcast.314, s32[3072]{0:T(1024)S(1)} %broadcast_clamp_fusion), kind=kCustom, calls=%fused_computation.3 | custom fusion | bytes 50343936 | tf_op jit(solution)/shard_map/gather | solution.py:298
  1230.9 28.5 %reshape.465 = f32[512,6,2048]{2,1,0:T(8,128)} reshape(f32[3072,2048]{1,0:T(8,128)} %gather_fusion.3) | data formatting | bytes 50331648 | tf_op jit(solution)/shard_map/reshape | solution.py:299
  1259.4 17.9 reduce_sum.143
  1277.3 8.3 bitcast_add_fusion.1
  1287.4 18.1 convolution_convert_fusion
  1305.5 31.0 %copy.151 = bf16[2,2048,2048]{2,0,1:T(2,128)(2,1)} copy(bf16[2,2048,2048]{2,1,0:T(8,128)(2,1)} %convolution_convert_fusion) | data formatting | bytes 33554432 | tf_op jit(solution)/shard_map/convert_element_type | solution.py:59
  1336.5 5.9 all-to-all-start.3
  1342.4 95.6 %all-reduce.12.cloned.1.call-done = f32[2,256,2048]{2,1,0:T(8,128)} async-done(((f32[2,256,2048]{2,1,0:T(8,128)}), f32[2,256,2048]{2,1,0:T(8,128)}) %all-reduce.12.cloned.1.call-update) | async-done | bytes 4194320 | tf_op jit(solution)/shard_map/psum | solution.py:302
  1438.0 5.2 multiply_reduce_fusion.2
  1449.5 5.7 multiply_reduce_fusion.1
  1475.5 5.3 bitcast_convert_fusion.3
  1486.1 52.8 %all-to-all-done.3 = bf16[2,2048,2048]{2,0,1:T(2,128)(2,1)} async-done(((bf16[2,2048,2048]{2,0,1:T(2,128)(2,1)}), bf16[2,2048,2048]{2,0,1:T(2,128)(2,1)}, u32[]{:S(2)}, u32[]{:S(2)}) %all-to-all-start.3) | async-done | bytes 16777248 | tf_op jit(solution)/shard_map/all_to_all | solution.py:237
  1538.9 20.1 %copy.152 = f32[2,8,256,2048]{3,2,0,1:T(8,128)} copy(bf16[2,8,256,2048]{3,0,2,1:T(2,128)(2,1)} %bitcast.88) | data formatting | bytes 50331648 | tf_op jit(solution)/shard_map/convert_element_type | solution.py:243
  1559.1 34.8 %gather_fusion.1 = f32[3072,2048]{1,0:T(8,128)} fusion(f32[4096,2048]{1,0:T(8,128)} %bitcast.313, s32[3072]{0:T(1024)S(1)} %broadcast_clamp_fusion), kind=kCustom, calls=%fused_computation.1 | custom fusion | bytes 50343936 | tf_op jit(solution)/shard_map/gather | solution.py:275
  1593.9 28.8 %reshape.461 = f32[512,6,2048]{2,1,0:T(8,128)} reshape(f32[3072,2048]{1,0:T(8,128)} %gather_fusion.1) | data formatting | bytes 50331648 | tf_op jit(solution)/shard_map/reshape | solution.py:275
  1622.7 17.8 multiply_reduce_fusion
  1653.4 5.9 bitcast_convert_fusion.6
  1664.3 14.4 fusion.48
  1678.7 5.8 copy.171
  1689.3 18.2 convert_bitcast_fusion.2
  1707.4 16.1 copy.169
  1741.6 7.0 convert_bitcast_fusion.1
  1748.5 10.2 copy.172
  1758.8 66.2 %all-reduce.14.cloned.1.call-done = (bf16[2,256,2048]{2,1,0:T(8,128)(2,1)}, bf16[2,256,2048]{2,1,0:T(8,128)(2,1)}, bf16[2,256,64]{1,2,0:T(8,128)(2,1)}, bf16[2,256,512]{1,2,0:T(8,128)(2,1)}) async-done(((bf16[2,256,2048]{2,1,0:T(8,128)(2,1)}, bf16[2,256,2048]{2,1,0:T(8,128)(2,1)}, bf16[2,256,64]{1,2,0:T(8,128)(2,1)}, bf16[2,256,512]{1,2,0:T(8,128)(2,1)}), (bf16[2,256,2048]{2,1,0:T(8,128)(2,1)}, ...) | async-done | bytes 4784144 | tf_op jit(solution)/shard_map/psum | solution.py:278
  1832.4 9.3 convert_bitcast_fusion
  1841.6 19.1 copy.170
  1864.9 43.1 %reduce-scatter.19.cloned.1.call-done = bf16[512,256]{1,0:T(8,128)(2,1)} async-done(((bf16[512,2048]{1,0:T(8,128)(2,1)}), bf16[512,256]{1,0:T(8,128)(2,1)}) %reduce-scatter.19.cloned.1.call-update) | async-done | bytes 262160 | tf_op jit(solution)/shard_map/reduce_scatter | solution.py:414
  1909.8 47.7 %reduce-scatter.13.cloned.1.call-done = bf16[256,768]{1,0:T(8,128)(2,1)} async-done(((bf16[2048,768]{1,0:T(8,128)(2,1)}), bf16[256,768]{1,0:T(8,128)(2,1)}) %reduce-scatter.13.cloned.1.call-update) | async-done | bytes 393232 | tf_op jit(solution)/shard_map/reduce_scatter | solution.py:402
  1959.4 7.0 fusion.36
  1966.4 13.3 all-reduce.4
  1980.9 8.8 fusion.33
  1989.7 13.9 reduce-scatter.15.cloned.1.call-done
  (316 shorter events, 160.1 us)
Async XLA Ops:
  7.2 211.9 %all-gather.10.cloned.1.call-start = ((), (), s32[]{:S(2)}) async-start(), calls=%async_computation.16 | async-start | bytes 2654208 | tf_op jit(solution)/shard_map/all_gather | solution.py:105
  7.9 433.1 %all-gather.16.cloned.1.call-start = ((), (), s32[]{:S(2)}) async-start(), calls=%async_computation.19 | async-start | bytes 3538944 | tf_op jit(solution)/shard_map/all_gather | solution.py:104
  8.7 12.3 copy-start.71
  8.7 49.7 %all-to-all-start.2 = ((bf16[256,16,352]{0,2,1:T(8,128)(2,1)}), bf16[256,16,352]{0,2,1:T(8,128)(2,1)S(1)}, u32[]{:S(2)}, u32[]{:S(2)}) async-start(bf16[256,16,352]{0,2,1:T(8,128)(2,1)} %param.31), calls=%async_computation.2 | async-start | bytes 5767168 | tf_op jit(solution)/shard_map/all_to_all | solution.py:225
  13.9 432.3 %all-gather.14.cloned.1.call-start = ((), (), s32[]{:S(2)}) async-start(), calls=%async_computation.18 | async-start | bytes 1179648 | tf_op jit(solution)/shard_map/all_gather | solution.py:107
  21.0 43.8 %copy-start.62 = (f32[2,256]{1,0:T(2,128)}, f32[2,256]{1,0:T(2,128)S(1)}, u32[]{:S(2)}) copy-start(f32[2,256]{1,0:T(2,128)S(1)} %compare_convert_fusion) | copy-start | bytes 6148
  21.0 453.4 %copy-start.50 = (s32[3072,1]{0,1:T(1,128)}, s32[3072,1]{0,1:T(1,128)S(1)}, u32[]{:S(2)}) copy-start(s32[3072,1]{0,1:T(1,128)S(1)} %compare_select_fusion) | copy-start | bytes 36868
  59.9 181.7 %all-to-all-start.1 = ((bf16[256,16,2,352]{0,3,2,1:T(8,128)(2,1)}), bf16[256,16,2,352]{0,3,2,1:T(8,128)(2,1)}, u32[]{:S(2)}, u32[]{:S(2)}) async-start(bf16[256,16,2,352]{0,3,2,1:T(8,128)(2,1)} %param.30), calls=%async_computation.1 | async-start | bytes 11534336 | tf_op jit(solution)/shard_map/all_to_all | solution.py:224
  64.7 81.6 %copy-start.72 = (u32[32]{0:T(128)S(1)}, u32[32]{0:T(128)}, u32[]{:S(2)}) copy-start(u32[32]{0:T(128)} %constant.69) | copy-start | bytes 388
  64.7 82.8 %copy-start.78 = (bf16[64]{0:T(256)(128)(2,1)S(1)}, bf16[64]{0:T(256)(128)(2,1)}, u32[]{:S(2)}) copy-start(bf16[64]{0:T(256)(128)(2,1)} %param.24) | copy-start | bytes 388
  64.7 95.3 %copy-start.65 = (f32[2,256,6]{1,0,2:T(2,128)S(1)}, f32[2,256,6]{1,0,2:T(2,128)}, u32[]{:S(2)}) copy-start(f32[2,256,6]{1,0,2:T(2,128)} %param.19) | copy-start | bytes 36868
  64.7 381.5 %all-gather.12.cloned.1.call-start = ((), (), s32[]{:S(2)}) async-start(), calls=%async_computation.17 | async-start | bytes 2621440 | tf_op jit(solution)/shard_map/all_gather | solution.py:144
  146.3 294.7 %copy-start.52 = (f32[8,1,256]{2,1,0:T(1,128)}, f32[8,1,256]{2,1,0:T(1,128)S(1)}, u32[]{:S(2)}) copy-start(f32[8,1,256]{2,1,0:T(1,128)S(1)} %convert_element_type.351) | copy-start | bytes 24580
  160.0 63.1 %copy-start.56 = (f32[512]{0:T(512)}, f32[512]{0:T(512)S(1)}, u32[]{:S(2)}) copy-start(f32[512]{0:T(512)S(1)} %convert_element_type.266) | copy-start | bytes 6148
  160.2 23.8 %copy-start.23 = (f32[2,256,6]{2,1,0:T(8,128)}, f32[2,256,6]{2,1,0:T(8,128)S(1)}, u32[]{:S(2)}) copy-start(f32[2,256,6]{2,1,0:T(8,128)S(1)} %copy.192) | copy-start | bytes 36868
  184.0 34.0 %copy-start.7 = (bf16[2,256,2048]{2,1,0:T(8,128)(2,1)S(1)}, bf16[2,256,2048]{2,1,0:T(8,128)(2,1)}, u32[]{:S(2)}) copy-start(bf16[2,256,2048]{2,1,0:T(8,128)(2,1)} %param.16) | copy-start | bytes 6291460
  219.1 221.9 %copy-start.67 = (f32[2,256]{1,0:T(2,128)}, f32[2,256]{1,0:T(2,128)S(1)}, u32[]{:S(2)}) copy-start(f32[2,256]{1,0:T(2,128)S(1)} %get-tuple-element.42) | copy-start | bytes 6148
  222.2 27.4 %copy-start.11 = (f32[2,256,576]{1,2,0:T(8,128)}, f32[2,256,576]{1,2,0:T(8,128)S(1)}, u32[]{:S(2)}) copy-start(f32[2,256,576]{1,2,0:T(8,128)S(1)} %fusion.58) | copy-start | bytes 3538948
  223.1 18.6 copy-start.54
  241.7 419.6 %all-to-all-start.4 = ((bf16[16,256,2048]{2,1,0:T(8,128)(2,1)}), bf16[16,256,2048]{2,1,0:T(8,128)(2,1)}, u32[]{:S(2)}, u32[]{:S(2)}) async-start(bf16[16,256,2048]{2,1,0:T(8,128)(2,1)} %multiply_convert_fusion), calls=%async_computation.4 | async-start | bytes 33554432 | tf_op jit(solution)/shard_map/all_to_all | solution.py:231
  247.4 213.0 %all-gather.18.cloned.1.call-start = ((), (), s32[]{:S(2)}) async-start(), calls=%async_computation.20 | async-start | bytes 2359296 | tf_op jit(solution)/shard_map/all_gather | solution.py:108
  248.0 373.1 %all-reduce.10.cloned.1.call-start = ((), (), s32[]{:S(2)}) async-start(), calls=%async_computation.21 | async-start | bytes 8388608 | tf_op jit(solution)/shard_map/psum | solution.py:175
  248.3 196.6 %copy-start.31 = (f32[256,32]{0,1:T(8,128)}, f32[256,32]{0,1:T(8,128)S(1)}, u32[]{:S(2)}) copy-start(f32[256,32]{0,1:T(8,128)S(1)} %get-tuple-element.47) | copy-start | bytes 98308
  248.3 196.6 %copy-start.33 = (f32[256,32]{0,1:T(8,128)}, f32[256,32]{0,1:T(8,128)S(1)}, u32[]{:S(2)}) copy-start(f32[256,32]{0,1:T(8,128)S(1)} %get-tuple-element.48) | copy-start | bytes 98308
  441.0 10.9 copy-start.21
  474.4 150.1 %copy-start.45 = (f32[8,1,256]{2,1,0:T(1,128)}, f32[8,1,256]{2,1,0:T(1,128)S(1)}, u32[]{:S(2)}) copy-start(f32[8,1,256]{2,1,0:T(1,128)S(1)} %convert_element_type.352) | copy-start | bytes 24580
  624.5 22.7 %copy-start.60 = (f32[2,256]{1,0:T(2,128)}, f32[2,256]{1,0:T(2,128)S(1)}, u32[]{:S(2)}) copy-start(f32[2,256]{1,0:T(2,128)S(1)} %get-tuple-element.46) | copy-start | bytes 6148
  626.3 355.9 %copy-start = (bf16[2,256,2048]{2,1,0:T(8,128)(2,1)}, bf16[2,256,2048]{2,1,0:T(8,128)(2,1)S(1)}, u32[]{:S(2)}) copy-start(bf16[2,256,2048]{2,1,0:T(8,128)(2,1)S(1)} %multiply_convert_fusion.4) | copy-start | bytes 6291460
  661.3 212.8 %all-to-all-start = ((bf16[16,256,2048]{2,1,0:T(8,128)(2,1)}), bf16[16,256,2048]{2,1,0:T(8,128)(2,1)}, u32[]{:S(2)}, u32[]{:S(2)}) async-start(bf16[16,256,2048]{2,1,0:T(8,128)(2,1)} %broadcast_multiply_fusion), calls=%async_computation | async-start | bytes 33554432 | tf_op jit(solution)/shard_map/all_to_all | solution.py:230
  667.0 315.2 %all-gather.20.cloned.1.call-start = ((), (), s32[]{:S(2)}) async-start(), calls=%async_computation.22 | async-start | bytes 6488064 | tf_op jit(solution)/shard_map/all_gather | solution.py:110
  975.3 201.4 %all-to-all-start.5 = ((bf16[2,2048,2048]{2,0,1:T(2,128)(2,1)}), bf16[2,2048,2048]{2,0,1:T(2,128)(2,1)}, u32[]{:S(2)}, u32[]{:S(2)}) async-start(bf16[2,2048,2048]{2,0,1:T(2,128)(2,1)} %copy.156), calls=%async_computation.5 | async-start | bytes 33554432 | tf_op jit(solution)/shard_map/all_to_all | solution.py:240
  981.2 115.6 %all-gather.22.cloned.1.call-start = ((), (), s32[]{:S(2)}) async-start(), calls=%async_computation.23 | async-start | bytes 3244032 | tf_op jit(solution)/shard_map/all_gather | solution.py:111
  981.9 456.0 %all-reduce.12.cloned.1.call-start = ((), (), s32[]{:S(2)}) async-start(), calls=%async_computation.24 | async-start | bytes 8388608 | tf_op jit(solution)/shard_map/psum | solution.py:302
  982.2 114.6 %copy-start.63 = (f32[2,256]{1,0:T(2,128)S(1)}, f32[2,256]{1,0:T(2,128)}, u32[]{:S(2)}) copy-start(f32[2,256]{1,0:T(2,128)} %copy-done.62) | copy-start | bytes 6148
  1103.2 174.1 %copy-start.37 = (bf16[2,256,1,704]{1,3,0,2:T(8,128)(2,1)}, bf16[2,256,1,704]{1,3,0,2:T(8,128)(2,1)S(1)}, u32[]{:S(2)}) copy-start(bf16[2,256,1,704]{1,3,0,2:T(8,128)(2,1)S(1)} %get-tuple-element.30) | copy-start | bytes 2162692
  1103.2 174.1 %copy-start.39 = (bf16[2,256,1,704]{1,3,0,2:T(8,128)(2,1)}, bf16[2,256,1,704]{1,3,0,2:T(8,128)(2,1)S(1)}, u32[]{:S(2)}) copy-start(bf16[2,256,1,704]{1,3,0,2:T(8,128)(2,1)S(1)} %get-tuple-element.31) | copy-start | bytes 2162692
  1336.4 101.5 %copy-start.46 = (f32[8,1,256]{2,1,0:T(1,128)S(1)}, f32[8,1,256]{2,1,0:T(1,128)}, u32[]{:S(2)}) copy-start(f32[8,1,256]{2,1,0:T(1,128)} %copy-done.45) | copy-start | bytes 24580
  1336.4 101.5 %copy-start.61 = (f32[2,256]{1,0:T(2,128)S(1)}, f32[2,256]{1,0:T(2,128)}, u32[]{:S(2)}) copy-start(f32[2,256]{1,0:T(2,128)} %copy-done.60) | copy-start | bytes 6148
  1336.4 106.7 %copy-start.14 = (bf16[2,256,2048]{2,1,0:T(8,128)(2,1)S(1)}, bf16[2,256,2048]{2,1,0:T(8,128)(2,1)}, u32[]{:S(2)}) copy-start(bf16[2,256,2048]{2,1,0:T(8,128)(2,1)} %param.20) | copy-start | bytes 6291460
  1336.5 202.5 %all-to-all-start.3 = ((bf16[2,2048,2048]{2,0,1:T(2,128)(2,1)}), bf16[2,2048,2048]{2,0,1:T(2,128)(2,1)}, u32[]{:S(2)}, u32[]{:S(2)}) async-start(bf16[2,2048,2048]{2,0,1:T(2,128)(2,1)} %copy.151), calls=%async_computation.3 | async-start | bytes 33554432 | tf_op jit(solution)/shard_map/all_to_all | solution.py:237
  1342.3 100.8 %copy-start.69 = (f32[2,256]{1,0:T(2,128)S(1)}, f32[2,256]{1,0:T(2,128)}, u32[]{:S(2)}) copy-start(f32[2,256]{1,0:T(2,128)} %get-tuple-element.45) | copy-start | bytes 6148
  1342.3 309.4 %reduce-scatter.11.cloned.1.call-start = ((), (), s32[]{:S(2)}) async-start(), calls=%async_computation.26 | async-start | bytes 327680 | tf_op jit(solution)/shard_map/reduce_scatter | solution.py:358
  1449.5 10.7 slice-start
  1449.5 10.7 slice-start.1
  1465.5 186.3 %reduce-scatter.9.cloned.1.call-start = ((), (), s32[]{:S(2)}) async-start(), calls=%async_computation.25 | async-start | bytes 2621440 | tf_op jit(solution)/shard_map/reduce_scatter | solution.py:355
  1475.4 262.0 %reduce-scatter.23.cloned.1.call-start = ((), (), s32[]{:S(2)}) async-start(), calls=%async_computation.32 | async-start | bytes 3244032 | tf_op jit(solution)/shard_map/reduce_scatter | solution.py:423
  1480.8 258.4 %reduce-scatter.21.cloned.1.call-start = ((), (), s32[]{:S(2)}) async-start(), calls=%async_computation.31 | async-start | bytes 6488064 | tf_op jit(solution)/shard_map/reduce_scatter | solution.py:420
  1485.9 339.0 %all-reduce.14.cloned.1.call-start = ((), (), s32[]{:S(2)}) async-start(), calls=%async_computation.33 | async-start | bytes 9568256 | tf_op jit(solution)/shard_map/psum | solution.py:278
  1593.9 28.8 %copy-start.24 = (f32[2,256,6]{2,1,0:T(8,128)S(1)}, f32[2,256,6]{2,1,0:T(8,128)}, u32[]{:S(2)}) copy-start(f32[2,256,6]{2,1,0:T(8,128)} %copy-done.23) | copy-start | bytes 36868
  1622.7 17.8 copy-start.74
  1622.7 17.8 copy-start.80
  1651.8 211.5 %reduce-scatter.17.cloned.1.call-start = ((), (), s32[]{:S(2)}) async-start(), calls=%async_computation.29 | async-start | bytes 1179648 | tf_op jit(solution)/shard_map/reduce_scatter | solution.py:411
  1659.3 248.8 %reduce-scatter.19.cloned.1.call-start = ((), (), s32[]{:S(2)}) async-start(), calls=%async_computation.30 | async-start | bytes 2359296 | tf_op jit(solution)/shard_map/reduce_scatter | solution.py:414
  1684.5 42.6 %all-to-all-start.7 = ((bf16[2048,2,352]{2,1,0:T(2,128)(2,1)}), bf16[2048,2,352]{2,1,0:T(2,128)(2,1)}, u32[]{:S(2)}, u32[]{:S(2)}) async-start(bf16[2048,2,352]{2,1,0:T(2,128)(2,1)} %copy.171), calls=%async_computation.15 | async-start | bytes 6291456 | tf_op jit(solution)/shard_map/all_to_all | solution.py:262
  1723.5 8.4 copy-start.68
  1727.1 105.2 %all-to-all-start.6 = ((bf16[2048,2,2,352]{3,2,1,0:T(2,128)(2,1)}), bf16[2048,2,2,352]{3,2,1,0:T(2,128)(2,1)}, u32[]{:S(2)}, u32[]{:S(2)}) async-start(bf16[2048,2,2,352]{3,2,1,0:T(2,128)(2,1)} %copy.169), calls=%async_computation.14 | async-start | bytes 12582912 | tf_op jit(solution)/shard_map/all_to_all | solution.py:255
  1731.9 225.6 %reduce-scatter.13.cloned.1.call-start = ((), (), s32[]{:S(2)}) async-start(), calls=%async_computation.27 | async-start | bytes 3538944 | tf_op jit(solution)/shard_map/reduce_scatter | solution.py:402
  1735.7 267.8 %reduce-scatter.15.cloned.1.call-start = ((), (), s32[]{:S(2)}) async-start(), calls=%async_computation.28 | async-start | bytes 2654208 | tf_op jit(solution)/shard_map/reduce_scatter | solution.py:405
  1748.5 77.2 %copy-start.12 = (f32[2,256,576]{1,2,0:T(8,128)S(1)}, f32[2,256,576]{1,2,0:T(8,128)}, u32[]{:S(2)}) copy-start(f32[2,256,576]{1,2,0:T(8,128)} %copy-done.11) | copy-start | bytes 3538948
  1748.5 77.2 %copy-start.55 = (f32[2,256]{1,0:T(2,128)S(1)}, f32[2,256]{1,0:T(2,128)}, u32[]{:S(2)}) copy-start(f32[2,256]{1,0:T(2,128)} %copy-done.54) | copy-start | bytes 6148
  1748.5 77.2 %copy-start.57 = (f32[512]{0:T(512)S(1)}, f32[512]{0:T(512)}, u32[]{:S(2)}) copy-start(f32[512]{0:T(512)} %copy-done.56) | copy-start | bytes 6148
  1748.5 78.7 %copy-start.70 = (f32[2,256]{1,0:T(2,128)S(1)}, f32[2,256]{1,0:T(2,128)}, u32[]{:S(2)}) copy-start(f32[2,256]{1,0:T(2,128)} %get-tuple-element.43) | copy-start | bytes 6148
  1841.6 117.8 %copy-start.42 = (bf16[2,256,512]{1,2,0:T(8,128)(2,1)S(1)}, bf16[2,256,512]{1,2,0:T(8,128)(2,1)}, u32[]{:S(2)}) copy-start(bf16[2,256,512]{1,2,0:T(8,128)(2,1)} %copy-done.41) | copy-start | bytes 1572868
  1959.4 21.5 %copy-start.66 = (f32[2,256]{1,0:T(2,128)S(1)}, f32[2,256]{1,0:T(2,128)}, u32[]{:S(2)}) copy-start(f32[2,256]{1,0:T(2,128)} %get-tuple-element.41) | copy-start | bytes 6148
  (46 other events, 179.0 us)
Sparse Core Ops, SparseCore 0:
  9.9 47.9 all-gather.9
  59.8 62.7 all-gather.15
  124.5 34.7 all-gather.13
  224.2 22.3 all-gather.11
  249.8 107.7 all-gather.17
  465.6 155.3 all-reduce.9
  675.5 127.1 all-gather.19
  984.0 112.7 all-gather.21
  1285.7 152.1 all-reduce.11
  1465.6 20.5 reduce-scatter.10
  1488.8 42.7 reduce-scatter.8
  1534.9 44.9 reduce-scatter.22
  1584.3 58.9 reduce-scatter.20
  1651.9 172.9 all-reduce.13
  1828.3 34.9 reduce-scatter.16
  1866.8 41.2 reduce-scatter.18
  1911.3 46.1 reduce-scatter.12
  1961.1 42.4 reduce-scatter.14
where the time goes:
time: 2030 us; the launch traced here: 2010 us
  waiting for transfers between devices  827 us (41%)
  local copies, waits for them, and re-layouts  458 us (23%)
  blocking collectives  303 us (15%)
  matrix products  216 us (11%)
  other arithmetic  138 us (7%)
  starting transfers between devices  52.4 us (3%)
    all_gather x1, blocking collectives, local(): lax.all_gather(rope_low, 'ctx', axis=1, tiled=True)  191 us
    all_to_all x1, waiting for transfers between devices, local(): lax.all_to_all(send_inputs, ('fsdp', 'ctx'), split_axis=0, concat_axis=1,...  156 us
    psum x1, waiting for transfers between devices, local(): middle = input_f + lax.psum(attn_part, 'tp')  125 us
    all_gather x1, waiting for transfers between devices, local(): lax.all_gather(shared_down, ('fsdp', 'ctx'), axis=1, tiled=True)  107 us
    psum x1, waiting for transfers between devices, local(): lax.psum(d_shared_in + d_routed_in.reshape(seq_dev, block, width), 'tp')  95.6 us
    all_gather x1, blocking collectives, local(): lax.all_gather(attn_gain, ('fsdp', 'ctx'), axis=0, tiled=True)  77.5 us
    all_to_all x1, waiting for transfers between devices, local(): lax.all_to_all(in_parts[:, :, 0], ('fsdp', 'ctx'), split_axis=1, concat_a...  73.5 us
    psum x1, waiting for transfers between devices, local(): lax.psum(moe_part.astype(jnp.bfloat16), 'tp').astype(jnp.float32)  66.2 us
  transfers between devices with their start and end apart: 26, of which 13 were waited for; matrix products, arithmetic and copies ran while one was open for 33% of the time, Pallas kernels for 0%

commit v1 on v0

v1 whole, which is shorter than its diff:
```python
import functools

import jax
import jax.numpy as jnp
from jax import lax
from jax.experimental import pallas as pl
from jax.experimental.pallas import tpu as pltpu
from jax.sharding import PartitionSpec as P

NOPE = 128
ROPE = 64
VDIM = 128
RANK = 512
TOP = 6
EXPERTS = 16
EPS = 1e-06
PLANE = ("fsdp", "ctx")
BF = jnp.bfloat16
F32 = jnp.float32


def rms_scale(values):
    return lax.rsqrt(jnp.mean(values * values, axis=-1, keepdims=True) + EPS)


def rotate(values, cosine, sine):
    half = values.shape[-1] // 2
    first = values[..., :half]
    second = values[..., half:]
    return jnp.concatenate([first * cosine - second * sine, first * sine + second * cosine], -1)


def rotate_back(grads, cosine, sine):
    half = grads.shape[-1] // 2
    first = grads[..., :half]
    second = grads[..., half:]
    return jnp.concatenate([first * cosine + second * sine, second * cosine - first * sine], -1)


def norm_back(values, scale, gain, grads):
    weighted = gain * grads
    return scale * weighted - values * (scale * scale * scale) * jnp.mean(
        weighted * values, axis=-1, keepdims=True
    )


def silu_parts(pre):
    sigma = jax.nn.sigmoid(pre)
    return (pre * sigma, sigma * (1.0 + pre * (1.0 - sigma)))


def dot(spec, a, b):
    return jnp.einsum(spec, a, b, preferred_element_type=F32)


def chip_shift(value, folds, chips_x, df, dx):
    if df == 0 and dx == 0:
        return value
    width = 2 * chips_x
    pairs = []
    for f in range(folds):
        for x in range(chips_x):
            for core in range(2):
                pairs.append(
                    (
                        f * width + 2 * x + core,
                        ((f + df) % folds) * width + 2 * ((x + dx) % chips_x) + core,
                    )
                )
    return lax.ppermute(value, PLANE, pairs)


def core_swap(value, folds, chips_x):
    count = folds * 2 * chips_x
    return lax.ppermute(value, PLANE, [(i, i ^ 1) for i in range(count)])


def first_hops(value, folds, chips_x, along=None):
    got = {}
    for df in range(folds):
        for dx in range(chips_x):
            if along is not None and dx == 0:
                got[df, dx] = along[df]
            elif df == 0 or dx == 0:
                got[df, dx] = chip_shift(value, folds, chips_x, df, dx)
    return got


def second_hops(got, folds, chips_x):
    half = got[0, 0].shape[-1] // 2
    for df in range(1, folds):
        for dx in range(1, chips_x):
            got[df, dx] = jnp.concatenate(
                [
                    chip_shift(got[0, dx][..., :half], folds, chips_x, df, 0),
                    chip_shift(got[df, 0][..., half:], folds, chips_x, 0, dx),
                ],
                -1,
            )
    return [got[df, dx] for df in range(folds) for dx in range(chips_x)]

def pieces_for(value, folds, chips_x):
    fold_at, ctx_at = lax.axis_index("fsdp"), lax.axis_index("ctx")
    for df in range(folds):
        for dx in range(chips_x):
            to = ((fold_at + df) % folds) * chips_x + (ctx_at // 2 + dx) % chips_x
            yield lax.dynamic_index_in_dim(value, to, 0, False), df, dx


def row_gather(value, folds, chips_x):
    got = jnp.stack([chip_shift(value, folds, chips_x, 0, dx) for dx in range(chips_x)])
    return jnp.concatenate([got, core_swap(got, folds, chips_x)])


def row_reduce(parts, folds, chips_x):
    both = parts[:chips_x].astype(F32) + core_swap(parts[chips_x:], folds, chips_x).astype(F32)
    total = both[0]
    for dx in range(1, chips_x):
        total = total + chip_shift(both[dx].astype(BF), folds, chips_x, 0, -dx).astype(F32)
    return total


def plane_reduce(parts, folds, chips_x):
    chips = folds * chips_x
    both = parts[:chips].astype(F32) + core_swap(parts[chips:], folds, chips_x).astype(F32)
    both = both.astype(BF)
    total = None
    for df in range(folds):
        for dx in range(chips_x):
            one = chip_shift(both[df * chips_x + dx], folds, chips_x, -df, -dx).astype(F32)
            total = one if total is None else total + one
    return total


def dot_nn(a, b):
    return lax.dot_general(a, b, (((1,), (0,)), ((), ())), preferred_element_type=F32)


def dot_nt(a, b):
    return lax.dot_general(a, b, (((1,), (1,)), ((), ())), preferred_element_type=F32)


def dot_tn(a, b):
    return lax.dot_general(a, b, (((0,), (0,)), ((), ())), preferred_element_type=F32)


class Sizes:
    def __init__(self, chips, per_chip, units, part, seqs, block, width):
        self.chips, self.per_chip, self.units, self.part = chips, per_chip, units, part
        self.seqs, self.block, self.width = seqs, block, width
        self.tokens = seqs * block
        self.capacity = block // 2
        self.slots = seqs * self.capacity
        self.row_a = per_chip * 2 * units
        self.row_b = self.row_a + per_chip * units
        self.row_c = self.row_b + 2 * part
        self.rows = self.row_c + part


def placement(sizes, code_ref, at):
    span = pl.ds(at * sizes.block, sizes.block)
    index = lax.broadcasted_iota(jnp.int32, (sizes.capacity, sizes.block), 0).astype(F32)
    rows = [
        jnp.where(code_ref[e : e + 1, span] == index, 1.0, 0.0) for e in range(sizes.per_chip)
    ]
    return jnp.concatenate(rows, 0)


def slot_gates(sizes, place, gate_ref, at):
    span = pl.ds(at * sizes.block, sizes.block)
    cap = sizes.capacity
    columns = [
        jnp.sum(place[e * cap : (e + 1) * cap] * gate_ref[e : e + 1, span], -1, keepdims=True)
        for e in range(sizes.per_chip)
    ]
    return jnp.concatenate(columns, 0)


def chunk_kernel(sizes, straight, *refs):
    code_ref, gate_ref, x_ref, g_ref = refs[:4]
    count = 2 * sizes.chips if straight else 1
    weight_refs, refs = refs[4 : 4 + count], refs[-9:]
    (in_ref, out_ref, acts_ref, shared_ref, w_ref, xs_ref, gs_ref, gate_cols, sems) = refs
    units, part, cap = sizes.units, sizes.part, sizes.capacity
    copies = []
    if straight:
        piece = weight_refs[0].shape[1]
        fold_at, ctx_at = lax.axis_index("fsdp"), lax.axis_index("ctx")
        folds, chips_x = lax.axis_size("fsdp"), lax.axis_size("ctx") // 2
        core = lax.rem(ctx_at, 2)
        for j, source in enumerate(weight_refs):
            df, dx = j % sizes.chips // chips_x, j % chips_x
            chip = lax.rem(fold_at + folds - df, folds) * chips_x + lax.rem(
                ctx_at // 2 + chips_x - dx, chips_x
            )
            side = core if j < sizes.chips else 1 - core
            column = pl.multiple_of((2 * chip + side) * piece, piece)
            copies.append(
                pltpu.make_async_copy(source, w_ref.at[:, pl.ds(column, piece)], sems.at[j])
            )
    else:
        copies.append(pltpu.make_async_copy(weight_refs[0], w_ref, sems.at[0]))
    for copy in copies:
        copy.start()
    for at in range(sizes.seqs):
        place = placement(sizes, code_ref, at)
        gates = slot_gates(sizes, place, gate_ref, at)
        place = place.astype(BF)
        span = pl.ds(at * sizes.block, sizes.block)
        rows_in = dot_nn(place, x_ref[span, :]).astype(BF)
        rows_grad = (dot_nn(place, g_ref[span, :]) * gates).astype(BF)
        for e in range(sizes.per_chip):
            xs_ref[e, at] = rows_in[e * cap : (e + 1) * cap]
            gs_ref[e, at] = rows_grad[e * cap : (e + 1) * cap]
            gate_cols[e, at] = jnp.broadcast_to(
                gates[e * cap : (e + 1) * cap], gate_cols.shape[2:]
            )
    for copy in copies:
        copy.wait()

    def one_expert(e):
        top, low = e * 2 * units, e * units
        gate_up = w_ref[pl.ds(top, 2 * units), :]
        down = w_ref[pl.ds(sizes.row_a + low, units), :]
        rows_in = xs_ref[e].reshape(sizes.slots, sizes.width)
        rows_grad = gs_ref[e].reshape(sizes.slots, sizes.width)
        pre = dot_nt(gate_up, rows_in)
        d_hidden = dot_nt(down, rows_grad)
        act, slope = silu_parts(pre[:units])
        up = pre[units:]
        hidden = (act * up).astype(BF)
        d_gu = jnp.concatenate([d_hidden * up * slope, d_hidden * act], 0).astype(BF)
        acts_ref[pl.ds(top, 2 * units), :] = d_gu
        acts_ref[pl.ds(sizes.row_a + low, units), :] = hidden
        back = dot_tn(d_gu, gate_up).astype(BF)
        xs_ref[e] = back.reshape(sizes.seqs, cap, sizes.width)
        gates = gate_cols[e].reshape(sizes.slots, gate_cols.shape[3])[:, :1]
        ahead = (dot_tn(hidden, down) * gates).astype(BF)
        gs_ref[e] = ahead.reshape(sizes.seqs, cap, sizes.width)

    for e in range(sizes.per_chip):
        one_expert(e)
    s_gate_up = w_ref[sizes.row_b : sizes.row_c, :]
    s_down = w_ref[sizes.row_c :, :]
    for at in range(sizes.seqs):
        span = pl.ds(at * sizes.block, sizes.block)
        pre = dot_nt(s_gate_up, x_ref[span, :])
        d_hidden = dot_nt(s_down, g_ref[span, :])
        act, slope = silu_parts(pre[:part])
        up = pre[part:]
        hidden = (act * up).astype(BF)
        d_gu = jnp.concatenate([d_hidden * up * slope, d_hidden * act], 0).astype(BF)
        shared_ref[: 2 * part, span] = d_gu
        shared_ref[2 * part :, span] = hidden
        place = placement(sizes, code_ref, at).astype(BF)
        back = jnp.concatenate([xs_ref[e, at] for e in range(sizes.per_chip)], 0)
        in_ref[span, :] = (dot_tn(place, back) + dot_tn(d_gu, s_gate_up)).astype(BF)
        ahead = jnp.concatenate([gs_ref[e, at] for e in range(sizes.per_chip)], 0)
        out_ref[span, :] = (dot_tn(place, ahead) + dot_tn(hidden, s_down)).astype(BF)


def chunk_call(sizes, number, weights, code, gate, x_rows, g_rows, saved):
    straight = len(weights) > 1
    whole = lambda shape: pl.BlockSpec(shape, lambda i: (0,) * len(shape), pipeline_mode=pl.Buffered(1))
    anywhere = pl.BlockSpec(memory_space=pl.ANY)
    rows = (sizes.tokens, sizes.width)
    first = 4 + len(weights)
    saved = [] if saved is None else list(saved)
    acts_shape = (sizes.row_b, sizes.chips * sizes.slots)
    shared_shape = (3 * sizes.part, sizes.chips * sizes.tokens)
    flops = 2 * sizes.width * (
        6 * sizes.per_chip * 2 * sizes.units * sizes.slots // 2
        + 6 * sizes.part * sizes.tokens
        + 4 * sizes.per_chip * sizes.slots * sizes.block
    )
    return pl.pallas_call(
        functools.partial(chunk_kernel, sizes, straight),
        grid=(1,),
        in_specs=[whole(code.shape), whole(gate.shape), whole(rows), whole(rows)]
        + [anywhere] * (len(weights) + len(saved)),
        out_specs=[
            whole(rows),
            whole(rows),
            pl.BlockSpec((acts_shape[0], sizes.slots), lambda i: (0, number)),
            pl.BlockSpec((shared_shape[0], sizes.tokens), lambda i: (0, number)),
        ],
        out_shape=[
            jax.ShapeDtypeStruct(rows, BF),
            jax.ShapeDtypeStruct(rows, BF),
            jax.ShapeDtypeStruct(acts_shape, BF),
            jax.ShapeDtypeStruct(shared_shape, BF),
        ],
        scratch_shapes=[
            pltpu.VMEM((sizes.rows, sizes.width), BF),
            pltpu.VMEM((sizes.per_chip, sizes.seqs, sizes.capacity, sizes.width), BF),
            pltpu.VMEM((sizes.per_chip, sizes.seqs, sizes.capacity, sizes.width), BF),
            pltpu.VMEM((sizes.per_chip, sizes.seqs, sizes.capacity, 128), F32),
            pltpu.SemaphoreType.DMA((2 * sizes.chips,)),
        ],
        input_output_aliases={first: 2, first + 1: 3} if saved else {},
        compiler_params=pltpu.CompilerParams(vmem_limit_bytes=60 * 1024 * 1024),
        cost_estimate=pl.CostEstimate(
            flops=flops, bytes_accessed=2 * sizes.rows * sizes.width, transcendentals=0
        ),
        name="expert_rows",
    )(code, gate, x_rows, g_rows, *weights, *saved)


def weight_grad_kernel(sizes, straight, *refs):
    count = sizes.chips
    code_ref, gate_ref, acts_ref, shared_ref = refs[:4]
    x_refs, g_refs = refs[4 : 4 + count], refs[4 + count : 4 + 2 * count]
    outs = refs[4 + 2 * count : -2]
    xs_ref, gs_ref = refs[-2:]
    units, part, cap = sizes.units, sizes.part, sizes.capacity
    core = lax.rem(lax.axis_index("ctx"), 2)

    def put(start, size, grad):
        if not straight:
            outs[0][pl.ds(start, size), :] = grad.astype(BF)
            return
        half = grad.shape[1] // 2
        low, high = grad[:, :half].astype(BF), grad[:, half:].astype(BF)
        outs[0][0, pl.ds(start, size), :] = jnp.where(core == 0, low, high)
        outs[1][0, pl.ds(start, size), :] = jnp.where(core == 0, high, low)

    for c in range(count):
        for at in range(sizes.seqs):
            place = placement(sizes, code_ref.at[c], at)
            gates = slot_gates(sizes, place, gate_ref.at[c], at)
            place = place.astype(BF)
            span = pl.ds(at * sizes.block, sizes.block)
            rows_in = dot_nn(place, x_refs[c][span, :]).astype(BF)
            rows_grad = (dot_nn(place, g_refs[c][span, :]) * gates).astype(BF)
            into = pl.ds(c * sizes.slots + at * cap, cap)
            for e in range(sizes.per_chip):
                xs_ref[e, into] = rows_in[e * cap : (e + 1) * cap]
                gs_ref[e, into] = rows_grad[e * cap : (e + 1) * cap]

    def one_expert(e):
        top, low = e * 2 * units, e * units
        put(top, 2 * units, dot_nn(acts_ref[pl.ds(top, 2 * units), :], xs_ref[e]))
        put(
            sizes.row_a + low,
            units,
            dot_nn(acts_ref[pl.ds(sizes.row_a + low, units), :], gs_ref[e]),
        )

    for e in range(sizes.per_chip):
        one_expert(e)
    d_gu_sum, down_sum = None, None
    for c in range(count):
        span = pl.ds(c * sizes.tokens, sizes.tokens)
        one = dot_nn(shared_ref[: 2 * part, span], x_refs[c][...])
        two = dot_nn(shared_ref[2 * part :, span], g_refs[c][...])
        d_gu_sum = one if d_gu_sum is None else d_gu_sum + one
        down_sum = two if down_sum is None else down_sum + two
    put(sizes.row_b, 2 * part, d_gu_sum)
    put(sizes.row_c, part, down_sum)


def weight_grad_call(sizes, rows_local, code, gate, acts, shared_acts, x_chunks, g_chunks):
    straight = rows_local % 128 == 0
    columns = 2 * rows_local if straight else 256
    steps = sizes.width // columns
    whole = lambda shape: pl.BlockSpec(shape, lambda j: (0,) * len(shape), pipeline_mode=pl.Buffered(1))
    cols = pl.BlockSpec((sizes.tokens, columns), lambda j: (0, j))
    if straight:
        out_specs = [pl.BlockSpec((1, sizes.rows, rows_local), lambda j: (j, 0, 0))] * 2
        out_shape = [jax.ShapeDtypeStruct((sizes.chips, sizes.rows, rows_local), BF)] * 2
    else:
        out_specs = [pl.BlockSpec((sizes.rows, columns), lambda j: (0, j))]
        out_shape = [jax.ShapeDtypeStruct((sizes.rows, sizes.width), BF)]
    slots = sizes.chips * sizes.slots
    flops = 2 * sizes.width * (
        3 * sizes.per_chip * sizes.units * slots
        + 3 * sizes.part * sizes.tokens * sizes.chips
        + 2 * sizes.per_chip * slots * sizes.block
    )
    return pl.pallas_call(
        functools.partial(weight_grad_kernel, sizes, straight),
        grid=(steps,),
        in_specs=[whole(code.shape), whole(gate.shape), whole(acts.shape), whole(shared_acts.shape)]
        + [cols] * (2 * sizes.chips),
        out_specs=out_specs,
        out_shape=out_shape,
        scratch_shapes=[
            pltpu.VMEM((sizes.per_chip, slots, columns), BF),
            pltpu.VMEM((sizes.per_chip, slots, columns), BF),
        ],
        compiler_params=pltpu.CompilerParams(vmem_limit_bytes=60 * 1024 * 1024),
        cost_estimate=pl.CostEstimate(
            flops=flops, bytes_accessed=4 * sizes.rows * sizes.width, transcendentals=0
        ),
        name="expert_weight_grads",
    )(code, gate, acts, shared_acts, *x_chunks, *g_chunks)


def block_columns(count, piece):
    if count == 1:
        return [0]
    fold_at, ctx_at = lax.axis_index("fsdp"), lax.axis_index("ctx")
    folds, chips_x = lax.axis_size("fsdp"), lax.axis_size("ctx") // 2
    core = lax.rem(ctx_at, 2)
    columns = []
    for side in (core, 1 - core):
        for df in range(folds):
            for dx in range(chips_x):
                chip = lax.rem(fold_at + folds - df, folds) * chips_x + lax.rem(
                    ctx_at // 2 + chips_x - dx, chips_x
                )
                columns.append(pl.multiple_of((2 * chip + side) * piece, piece))
    return columns


class Rows:
    def __init__(self, out_rows, query_cols, up_rows, info_rows):
        self.heads = out_rows // VDIM
        self.out = out_rows
        self.nope = out_rows + self.heads * NOPE
        self.query = out_rows + query_cols
        self.latent = self.query + RANK
        self.rope = self.latent + ROPE
        self.up = self.rope + up_rows
        self.info = self.up + info_rows
        self.total = self.info + 16


def lanes_of(shape):
    return lax.broadcasted_iota(jnp.int32, shape, 1)


def spread(mixed):
    turned = pltpu.roll(mixed, ROPE // 2, 1)
    even = lax.rem(lanes_of(mixed.shape) // (ROPE // 2), 2) == 0
    return jnp.where(even, mixed, turned), jnp.where(even, turned, mixed)


def mix(first, second):
    even = lax.rem(lanes_of(first.shape) // (ROPE // 2), 2) == 0
    return jnp.where(even, first, second)


def project_kernel(rows, count, hidden_ref, gain_ref, cos_ref, sin_ref, *refs):
    blocks = refs[:count]
    low_ref, nope_ref, rope_ref, keys_ref, latent_ref, q_ref, kr_ref, x_ref = refs[count:]
    piece = blocks[0].shape[1]
    x = hidden_ref[...].astype(F32)
    x_ref[...] = x * rms_scale(x)
    for j, column in enumerate(block_columns(count, piece)):
        span = pl.ds(column, piece)
        block = blocks[j]
        low = (x_ref[:, span] * block[rows.info : rows.info + 1, :].astype(F32)).astype(BF)
        low_ref[:, span] = low
        half = ROPE // 2
        first = block[rows.latent : rows.latent + half, :]
        second = block[rows.latent + half : rows.rope, :]
        query = dot_nt(low, block[rows.out : rows.query, :])
        latent = dot_nt(low, block[rows.query : rows.latent, :])
        rope = dot_nt(low, jnp.concatenate([first] * 4 + [second] * 4, 0))
        if j == 0:
            q_ref[...], latent_ref[...], kr_ref[...] = query, latent, rope
        else:
            q_ref[...] += query
            latent_ref[...] += latent
            kr_ref[...] += rope
    cosine, sine = cos_ref[...], sin_ref[...]
    wide = rows.nope - rows.out
    side = (rows.query - rows.nope) // 2
    nope_ref[...] = q_ref[:, :wide].astype(BF)
    first, second = q_ref[:, wide : wide + side], q_ref[:, wide + side :]
    rope_ref[:, :side] = (first * cosine - second * sine).astype(BF)
    rope_ref[:, side:] = (first * sine + second * cosine).astype(BF)
    first, second = kr_ref[:, :128], kr_ref[:, 128:]
    latent = latent_ref[...]
    keys_ref[:, :RANK] = (latent * rms_scale(latent) * gain_ref[...]).astype(BF)
    keys_ref[:, RANK:] = mix(first * cosine - second * sine, first * sine + second * cosine).astype(BF)


def whole_spec(shape, rows=None):
    if rows is not None:
        shape = (rows,) + tuple(shape[1:])
    return pl.BlockSpec(
        tuple(shape), lambda i: (0,) * len(shape), pipeline_mode=pl.Buffered(1)
    )


def one_step(body, name, inputs, outputs, scratch, flops, scalars=()):
    arrays = [item[0] if isinstance(item, tuple) else item for item in inputs]
    specs = [
        whole_spec(item[0].shape, item[1]) if isinstance(item, tuple) else whole_spec(item.shape)
        for item in inputs
    ]
    smem = [pl.BlockSpec(memory_space=pltpu.SMEM)] * len(scalars)
    return pl.pallas_call(
        body,
        grid=(1,),
        in_specs=smem + specs,
        out_specs=[whole_spec(shape) for shape, _ in outputs],
        out_shape=[jax.ShapeDtypeStruct(shape, kind) for shape, kind in outputs],
        scratch_shapes=scratch,
        compiler_params=pltpu.CompilerParams(vmem_limit_bytes=60 * 1024 * 1024),
        cost_estimate=pl.CostEstimate(flops=flops, bytes_accessed=8 << 20, transcendentals=0),
        name=name,
    )(*scalars, *arrays)


def head_mask(shape, h):
    return lax.rem(lanes_of(shape) // (ROPE // 2), 128 // (ROPE // 2)) == h


def key_mask(lengths_ref, s, block, n_ctx):
    ctx_at = lax.axis_index("ctx")
    chips_x = n_ctx // 2
    core = lax.rem(ctx_at, 2)
    at = ctx_at * block + lax.broadcasted_iota(jnp.int32, (block, block), 0)
    within = lax.broadcasted_iota(jnp.int32, (block, block), 1)
    parts = []
    for side in (core, 1 - core):
        for dx in range(chips_x):
            start = (2 * lax.rem(ctx_at // 2 + chips_x - dx, chips_x) + side) * block
            key = start + within
            parts.append((key <= at) & (key < lengths_ref[s]))
    return jnp.concatenate([jnp.where(part, 0.0, -1e30) for part in parts], 1)


def attend_kernel(rows, count, seqs, block, n_ctx, lengths_ref, nope_ref, rope_ref, keys_ref, up_ref, *refs):
    blocks = refs[:count]
    part_ref, att_ref, exp_ref, lse_ref, kr_ref = refs[count:]
    piece = blocks[0].shape[1]
    scale = float(NOPE + ROPE) ** (-0.5)
    for s in range(seqs):
        here = pl.ds(s * block, block)
        for j in range(n_ctx):
            at = pl.ds(j * block, block)
            exp_ref[s, at, :] = dot_nn(keys_ref[j, s, :, :RANK], up_ref[...]).astype(BF)
            first, second = spread(keys_ref[j, s, :, RANK:].astype(F32))
            kr_ref[at, :128] = first.astype(BF)
            kr_ref[at, 128:] = second.astype(BF)
        bias = key_mask(lengths_ref, s, block, n_ctx)
        lse = jnp.zeros((block, 128), F32)
        for h in range(rows.heads):
            k = exp_ref[s, :, h * (NOPE + VDIM) : h * (NOPE + VDIM) + NOPE]
            v = exp_ref[s, :, h * (NOPE + VDIM) + NOPE : (h + 1) * (NOPE + VDIM)]
            q = nope_ref[here, h * NOPE : (h + 1) * NOPE]
            qr = rope_ref[here, :]
            qr = jnp.where(head_mask(qr.shape, h), qr, jnp.zeros_like(qr))
            raw = (dot_nt(q, k) + dot_nt(qr, kr_ref[...])) * scale
            masked = jnp.where(bias < 0.0, bias, raw)
            peak = jnp.max(masked, axis=-1, keepdims=True)
            expo = jnp.exp(masked - peak)
            total = jnp.sum(expo, axis=-1, keepdims=True)
            probs = (expo / total).astype(BF)
            att_ref[here, h * VDIM : (h + 1) * VDIM] = dot_nn(probs, v).astype(BF)
            lse = jnp.where(lanes_of(lse.shape) == h, peak + jnp.log(total), lse)
        lse_ref[here, :] = lse
    for j, column in enumerate(block_columns(count, piece)):
        part_ref[:, pl.ds(column, piece)] = dot_nn(att_ref[...], blocks[j][: rows.out, :]).astype(BF)


def attend_back_kernel(rows, count, seqs, block, n_ctx, lengths_ref, branch_ref, nope_ref, rope_ref,
                       keys_ref, exp_ref, lse_ref, up_ref, cos_ref, sin_ref, *refs):
    blocks = refs[:count]
    dq_ref, din_ref, dkeys_ref, up_grad_ref, datt_ref, dexp_ref, kr_ref, dkr_ref, sum_ref = refs[count:]
    piece = blocks[0].shape[1]
    scale = float(NOPE + ROPE) ** (-0.5)
    columns = block_columns(count, piece)
    side = (rows.query - rows.nope) // 2
    wide = rows.nope - rows.out
    for j, column in enumerate(columns):
        one = dot_nt(branch_ref[:, pl.ds(column, piece)], blocks[j][: rows.out, :])
        if j == 0:
            sum_ref[...] = one
        else:
            sum_ref[...] += one
    datt_ref[...] = sum_ref[...].astype(BF)
    for s in range(seqs):
        here = pl.ds(s * block, block)
        for j in range(n_ctx):
            at = pl.ds(j * block, block)
            first, second = spread(keys_ref[j, s, :, RANK:].astype(F32))
            kr_ref[at, :128] = first.astype(BF)
            kr_ref[at, 128:] = second.astype(BF)
        bias = key_mask(lengths_ref, s, block, n_ctx)
        lse_all = lse_ref[here, :]
        dq_rope = jnp.zeros((block, 2 * side), F32)
        for h in range(rows.heads):
            low, high = h * (NOPE + VDIM), (h + 1) * (NOPE + VDIM)
            k = exp_ref[s, :, low : low + NOPE]
            v = exp_ref[s, :, low + NOPE : high]
            q = nope_ref[here, h * NOPE : (h + 1) * NOPE]
            qr = rope_ref[here, :]
            mine = head_mask(qr.shape, h)
            qr = jnp.where(mine, qr, jnp.zeros_like(qr))
            datt = datt_ref[here, h * VDIM : (h + 1) * VDIM]
            raw = (dot_nt(q, k) + dot_nt(qr, kr_ref[...])) * scale
            lse = jnp.sum(jnp.where(lanes_of(lse_all.shape) == h, lse_all, 0.0), -1, keepdims=True)
            probs = jnp.exp(jnp.where(bias < 0.0, bias, raw) - lse)
            d_probs = dot_nt(datt, v)
            d_scores = probs * (d_probs - jnp.sum(probs * d_probs, axis=-1, keepdims=True))
            d_scores = d_scores.astype(BF)
            dq_ref[here, h * NOPE : (h + 1) * NOPE] = (dot_nn(d_scores, k) * scale).astype(BF)
            dq_rope = dq_rope + jnp.where(mine, dot_nn(d_scores, kr_ref[...]), 0.0)
            dexp_ref[:, low : low + NOPE] = (dot_tn(d_scores, q) * scale).astype(BF)
            dexp_ref[:, low + NOPE : high] = dot_tn(probs.astype(BF), datt).astype(BF)
            one = dot_tn(d_scores, qr)
            if h == 0:
                dkr_ref[...] = one
            else:
                dkr_ref[...] += one
        cosine, sine = cos_ref[here, :], sin_ref[here, :]
        first, second = dq_rope[:, :side] * scale, dq_rope[:, side:] * scale
        dq_ref[here, wide : wide + side] = (first * cosine + second * sine).astype(BF)
        dq_ref[here, wide + side :] = (second * cosine - first * sine).astype(BF)
        for j in range(n_ctx):
            at = pl.ds(j * block, block)
            folded = []
            for part in (dkr_ref[at, :128], dkr_ref[at, 128:]):
                part = part + pltpu.roll(part, 64, 1)
                folded.append((part + pltpu.roll(part, 32, 1)) * scale)
            dkeys_ref[j, s, :, RANK:] = mix(folded[0], folded[1]).astype(BF)
            dkeys_ref[j, s, :, :RANK] = dot_nt(dexp_ref[at, :], up_ref[...]).astype(BF)
            one = dot_tn(keys_ref[j, s, :, :RANK], dexp_ref[at, :])
            if s == 0 and j == 0:
                up_grad_ref[...] = one
            else:
                up_grad_ref[...] += one
    for j, column in enumerate(columns):
        din_ref[:, pl.ds(column, piece)] = dot_nn(dq_ref[...], blocks[j][rows.out : rows.query, :]).astype(BF)


def attend_grads_kernel(rows, count, piece, att_ref, branch_ref, dq_ref, low_ref, out_ref):
    for j, column in enumerate(block_columns(count, piece)):
        span = pl.ds(column, piece)
        out_ref[j, : rows.out, :] = dot_tn(att_ref[...], branch_ref[:, span]).astype(BF)
        out_ref[j, rows.out :, :] = dot_tn(dq_ref[...], low_ref[:, span]).astype(BF)


def last_kernel(rows, count, hidden_ref, low_ref, dq_ref, dlat_ref, dmid_ref, *refs):
    blocks = refs[:count]
    grad_ref, packed_ref, dlow_ref = refs[count:]
    piece = blocks[0].shape[1]
    columns = block_columns(count, piece)
    x = hidden_ref[...].astype(F32)
    scale = rms_scale(x)
    d_rope = dlat_ref[:, RANK:]
    d_rope = jnp.where(lanes_of(d_rope.shape) < ROPE, d_rope, jnp.zeros_like(d_rope))
    mean = jnp.zeros_like(scale)
    extra = packed_ref.shape[1] - (RANK + ROPE)
    for j, column in enumerate(columns):
        span = pl.ds(column, piece)
        block = blocks[j]
        d_low = dq_ref[:, span].astype(F32) + dot_nn(dlat_ref[:, :RANK], block[rows.query : rows.latent, :])
        d_low = d_low + dot_nn(d_rope, block[rows.latent : rows.latent + 128, :])
        x_part = hidden_ref[:, span].astype(F32)
        weighted = d_low * block[rows.info : rows.info + 1, :].astype(F32)
        dlow_ref[:, span] = weighted
        mean = mean + jnp.sum(weighted * x_part, axis=-1, keepdims=True)
        gain_grad = jnp.sum(d_low * x_part * scale, axis=0, keepdims=True)
        top = lax.broadcasted_iota(jnp.int32, (extra, piece), 0) == 0
        packed_ref[j, RANK + ROPE :, :] = jnp.where(top, gain_grad, 0.0).astype(BF)
        packed_ref[j, : RANK + ROPE, :] = dot_tn(dlat_ref[...], low_ref[:, span])[: RANK + ROPE].astype(BF)
    mean = mean * (scale * scale * scale) / hidden_ref.shape[1]
    grad_ref[...] = dmid_ref[...] + scale * dlow_ref[...] - hidden_ref[...].astype(F32) * mean


def local(
    hidden_in,
    lengths,
    routes,
    gate_weights,
    cotangent,
    attn_gain,
    query_weight,
    latent_down,
    latent_gain,
    latent_up,
    output_weight,
    ffn_gain,
    shared_gate_up,
    shared_down,
    expert_gate_up,
    expert_down,
):
    seq_dev, block, width = hidden_in.shape
    tokens = seq_dev * block
    folds, n_ctx = lax.axis_size("fsdp"), lax.axis_size("ctx")
    chips_x = n_ctx // 2
    chips = folds * chips_x
    plane = folds * n_ctx
    rows_local = expert_gate_up.shape[0]
    units = expert_gate_up.shape[-1]
    shared_units = shared_down.shape[0]
    per_chip = EXPERTS // chips
    shared_part = shared_units // chips
    fold_at, ctx_at = lax.axis_index("fsdp"), lax.axis_index("ctx")
    core = ctx_at % 2
    chip_at = fold_at * chips_x + ctx_at // 2
    same_core = [
        [(f * n_ctx + 2 * x + k) for f in range(folds) for x in range(chips_x)] for k in range(2)
    ]

    positions = ctx_at * block + jnp.arange(block, dtype=jnp.int32)
    valid = (positions[None, :] < lengths[:, None]).astype(F32)
    grad_out = cotangent.astype(F32) * valid[:, :, None]
    grad_low = grad_out.astype(BF)

    sizes = Sizes(
        chips, per_chip, units, shared_part + -shared_part % 16, seq_dev, block, width
    )
    experts_t = expert_gate_up.transpose(1, 2, 3, 0).reshape(chips, sizes.row_a, rows_local)
    edown_t = expert_down.transpose(1, 2, 0).reshape(chips, sizes.row_b - sizes.row_a, rows_local)
    extra = ((0, 0), (0, 0), (0, sizes.part - shared_part), (0, 0))
    shared_t = (
        shared_gate_up.transpose(1, 2, 0)
        .reshape(2, chips, shared_part, rows_local)
        .transpose(1, 0, 2, 3)
    )
    shared_t = jnp.pad(shared_t, extra).reshape(chips, 2 * sizes.part, rows_local)
    sdown_t = jnp.pad(shared_down.reshape(chips, 1, shared_part, rows_local), extra)
    sdown_t = sdown_t.reshape(chips, sizes.part, rows_local)
    to_chips = jnp.concatenate([experts_t, edown_t, shared_t, sdown_t], 1)
    named = routes[..., None] == jnp.arange(EXPERTS, dtype=jnp.int32)
    mask = jnp.any(named, axis=2)
    gate_of = jnp.sum(jnp.where(named, gate_weights[..., None], 0.0), axis=2)
    earlier = (jnp.arange(block)[:, None] > jnp.arange(block)[None, :]).astype(BF)
    ranks = dot("ut,ste->sue", earlier, mask.astype(BF))
    code = jnp.where(mask, ranks, -1.0)
    gate_high = lax.reduce_precision(gate_of, 8, 7)
    gate_rest = gate_of - gate_high
    gate_mid = lax.reduce_precision(gate_rest, 8, 7)
    info = jnp.stack([code, gate_high, gate_mid, gate_rest - gate_mid]).astype(BF)
    info = info.transpose(3, 0, 1, 2).reshape(-1, rows_local)

    query_cols = query_weight.shape[1]
    down_cols = latent_down.shape[1]
    out_rows = output_weight.shape[0]
    rank_local = latent_up.shape[0]
    up_rows = rank_local * latent_up.shape[1] // rows_local
    heads_dev = query_cols // (NOPE + ROPE)
    rows = Rows(out_rows, query_cols, up_rows, info.shape[0])
    straight = rows_local % 128 == 0
    query_t = query_weight.T.reshape(heads_dev, NOPE + ROPE, rows_local)
    rope_t = query_t[:, NOPE:].reshape(heads_dev, 2, ROPE // 2, rows_local).transpose(1, 0, 2, 3)
    gains = jnp.stack([attn_gain, ffn_gain, jnp.pad(latent_gain, (0, rows_local - rank_local))])
    packed = jnp.concatenate(
        [
            output_weight,
            query_t[:, :NOPE].reshape(heads_dev * NOPE, rows_local),
            rope_t.reshape(heads_dev * ROPE, rows_local),
            latent_down.T,
            latent_up.reshape(up_rows, rows_local),
            info,
            jnp.pad(gains, ((0, 13), (0, 0))),
        ],
        0,
    )
    grad_rows = grad_low.reshape(tokens, width)
    own_blocks = first_hops(packed, folds, chips_x)
    own_blocks, to_chips, grad_rows = lax.optimization_barrier((own_blocks, to_chips, grad_rows))
    own_blocks = second_hops(own_blocks, folds, chips_x)
    blocks = own_blocks + [core_swap(one, folds, chips_x) for one in own_blocks]
    order = jnp.stack(
        [
            ((core != side).astype(jnp.int32) * folds + (fold_at - f) % folds) * chips_x
            + (ctx_at // 2 - x) % chips_x
            for f in range(folds)
            for x in range(chips_x)
            for side in range(2)
        ]
    )

    def in_order(parts):
        return jnp.take(jnp.stack(parts), order, axis=0)

    def by_shift(parts):
        came = jnp.stack(
            [
                2 * (((fold_at - df) % folds) * chips_x + (ctx_at // 2 - dx) % chips_x) + side
                for side in (core, 1 - core)
                for df in range(folds)
                for dx in range(chips_x)
            ]
        )
        return jnp.take(parts, came, axis=0)

    up_full = in_order([one[rows.rope : rows.up] for one in blocks])
    up_full = up_full.reshape(RANK, latent_up.shape[1])
    gain_all = in_order([one[rows.info : rows.info + 3] for one in blocks])
    gain_two = gain_all[:, 1].reshape(width).astype(F32)
    lat_gain = gain_all[:, 2, :rank_local].reshape(RANK).astype(F32)
    info_all = jnp.stack([one[rows.up : rows.info] for one in own_blocks])
    if not straight:
        blocks = [in_order(blocks).transpose(1, 0, 2).reshape(rows.total, width)]
    count, piece = len(blocks), blocks[0].shape[1]
    info_all = info_all.reshape(chips, EXPERTS, 4, tokens)
    info_all = lax.dynamic_slice_in_dim(info_all, chip_at * per_chip, per_chip, 1).astype(F32)
    info_all = jnp.pad(info_all, ((0, 0), (0, -per_chip % 8), (0, 0), (0, 0)))
    code_all = info_all[:, :, 0]
    gate_all = info_all[:, :, 1] + info_all[:, :, 2] + info_all[:, :, 3]

    total_len = block * n_ctx
    inverse = 10000.0 ** (-jnp.arange(ROPE // 2, dtype=F32) / (ROPE // 2))
    angles = positions.astype(F32)[:, None] * inverse[None, :]
    cosine = jnp.tile(jnp.cos(angles), (seq_dev, 4))
    sine = jnp.tile(jnp.sin(angles), (seq_dev, 4))
    hidden_rows = hidden_in.reshape(tokens, width)
    side = heads_dev * ROPE
    low_one, q_nope, q_rope, key_rows, latent = one_step(
        functools.partial(project_kernel, rows, count),
        "project",
        [hidden_rows, lat_gain[None], cosine, sine] + blocks,
        [
            ((tokens, width), BF),
            ((tokens, heads_dev * NOPE), BF),
            ((tokens, side), BF),
            ((tokens, RANK + 128), BF),
            ((tokens, RANK), F32),
        ],
        [
            pltpu.VMEM((tokens, query_cols), F32),
            pltpu.VMEM((tokens, 256), F32),
            pltpu.VMEM((tokens, width), F32),
        ],
        2 * tokens * width * (query_cols + RANK + 256),
    )
    keys_all = row_gather(key_rows.reshape(seq_dev, block, RANK + 128), folds, chips_x)
    pieces = list(pieces_for(to_chips, folds, chips_x))
    from_chips = {
        (df, dx): chip_shift(one, folds, chips_x, df, dx)
        for one, df, dx in pieces
        if df == 0 or dx == 0
    }
    g_along = [chip_shift(grad_rows, folds, chips_x, df, 0) for df in range(folds)]
    late = [one for one in pieces if one[1] != 0 and one[2] != 0]
    late, grad_again, keys_all, from_chips = lax.optimization_barrier(
        ([one for one, _, _ in late], grad_rows, keys_all, from_chips)
    )
    at_once = from_chips
    late = {
        (df, dx): chip_shift(one, folds, chips_x, df, dx)
        for one, (df, dx) in zip(late, [at[1:] for at in pieces if at[1] != 0 and at[2] != 0])
    }
    attn_part, attended, expanded, log_total = one_step(
        functools.partial(attend_kernel, rows, count, seq_dev, block, n_ctx),
        "attend",
        [q_nope, q_rope, keys_all, up_full] + [(one, rows.out) for one in blocks],
        [
            ((tokens, width), BF),
            ((tokens, out_rows), BF),
            ((seq_dev, total_len, up_full.shape[1]), BF),
            ((tokens, 128), F32),
        ],
        [pltpu.VMEM((total_len, 256), BF)],
        2 * tokens * total_len * (RANK * 4 + 384 * heads_dev),
        (lengths,),
    )
    attn_part = attn_part.reshape(seq_dev, block, width)
    input_f = hidden_in.astype(F32)
    attn_sum = lax.psum(attn_part, "tp")

    g_first = first_hops(grad_again, folds, chips_x, g_along)
    late, g_first, attn_sum = lax.optimization_barrier((late, g_first, attn_sum))
    swapped = {at: core_swap(one, folds, chips_x) for at, one in at_once.items()}
    swapped.update({at: core_swap(one, folds, chips_x) for at, one in late.items()})
    arrived = {**at_once, **late}
    shifts = [(df, dx) for df in range(folds) for dx in range(chips_x)]
    from_chips = [arrived[at] for at in shifts]
    from_other = [swapped[at] for at in shifts]
    if straight:
        chip_weights = tuple(from_chips + from_other)
    else:
        both = in_order(from_chips + from_other)
        chip_weights = (both.transpose(1, 0, 2).reshape(sizes.rows, width),)
    middle = input_f + attn_sum.astype(F32)
    scale_two = rms_scale(middle)
    low_two = (middle * scale_two * gain_two).astype(BF)

    in_parts, out_parts = [], []

    def run_chunk(number, x_rows, g_rows, saved):
        part_in, part_out, *saved = chunk_call(
            sizes,
            number,
            chip_weights,
            code_all[number],
            gate_all[number],
            x_rows,
            g_rows,
            saved,
        )
        in_parts.append(part_in)
        out_parts.append(part_out)
        return saved

    own_rows = low_two.reshape(tokens, width)
    x_first = first_hops(own_rows, folds, chips_x)
    saved = run_chunk(0, own_rows, g_first[0, 0], None)
    x_first, g_first, saved = lax.optimization_barrier((x_first, g_first, saved))
    x_chunks = second_hops(x_first, folds, chips_x)
    g_chunks = second_hops(g_first, folds, chips_x)
    for number in range(1, chips):
        saved = run_chunk(number, x_chunks[number], g_chunks[number], saved)
    acts, shared_acts = saved

    def send(parts):
        return [
            chip_shift(parts[df * chips_x + dx], folds, chips_x, -df, -dx)
            for df in range(folds)
            for dx in range(chips_x)
        ]

    def total(parts):
        return sum(part.astype(F32) for part in parts).astype(BF).reshape(seq_dev, block, width)

    in_home = send(in_parts)
    ffn_g = weight_grad_call(
        sizes, rows_local, code_all, gate_all, acts, shared_acts, x_chunks, g_chunks
    )
    in_home, ffn_g = lax.optimization_barrier((in_home, ffn_g))
    in_sum = total(in_home)
    d_low_two = lax.psum(in_sum, "tp")
    in_sum, out_parts = lax.optimization_barrier((in_sum, out_parts))
    moe_low = total(send(out_parts))

    if straight:
        kept, given = ffn_g
    else:
        both = ffn_g[0].reshape(sizes.rows, chips, 2, rows_local).transpose(2, 1, 0, 3)
        kept = lax.dynamic_index_in_dim(both, core, 0, False)
        given = lax.dynamic_index_in_dim(both, 1 - core, 0, False)
    given = core_swap(given, folds, chips_x)
    moe_low, d_low_two = lax.optimization_barrier((moe_low, d_low_two))
    d_low_two = d_low_two.astype(F32)
    ffn_gain_g = jnp.sum(d_low_two * middle * scale_two, axis=(0, 1))
    d_middle = grad_out + norm_back(middle, scale_two, gain_two, d_low_two)
    d_branch = d_middle.astype(BF)
    d_branch = d_branch.reshape(tokens, width)
    d_query_pre, d_query_in, d_keys_part, latent_up_g = one_step(
        functools.partial(attend_back_kernel, rows, count, seq_dev, block, n_ctx),
        "attend_back",
        [d_branch, q_nope, q_rope, keys_all, expanded, log_total, up_full, cosine, sine]
        + [(one, rows.query) for one in blocks],
        [
            ((tokens, query_cols), BF),
            ((tokens, width), BF),
            ((n_ctx, seq_dev, block, RANK + 128), BF),
            ((RANK, up_full.shape[1]), F32),
        ],
        [
            pltpu.VMEM((tokens, out_rows), BF),
            pltpu.VMEM((total_len, up_full.shape[1]), BF),
            pltpu.VMEM((total_len, 256), BF),
            pltpu.VMEM((total_len, 256), F32),
            pltpu.VMEM((tokens, out_rows), F32),
        ],
        4 * tokens * total_len * (RANK * 4 + 384 * heads_dev),
        (lengths,),
    )
    d_keys_ctx = row_reduce(d_keys_part, folds, chips_x).astype(BF)
    d_query_in, d_keys_ctx, kept, given = lax.optimization_barrier(
        (d_query_in, d_keys_ctx, kept, given)
    )
    d_keys, d_query_sum = lax.psum((d_keys_ctx, d_query_in), "tp")
    ffn_sum = (kept.astype(F32) + given.astype(F32)).astype(BF)
    ffn_home = lax.all_to_all(
        ffn_sum, PLANE, split_axis=0, concat_axis=0, axis_index_groups=same_core, tiled=True
    ).astype(F32)
    d_keys, d_query_sum, d_query_pre, moe_low = lax.optimization_barrier(
        (d_keys, d_query_sum, d_query_pre, moe_low)
    )
    moe_sum = lax.psum(moe_low, "tp")

    def relayed(parts):
        if straight:
            return parts
        return by_shift(parts[0].reshape(-1, plane, rows_local).transpose(1, 0, 2))

    d_keys = d_keys.reshape(tokens, RANK + 128).astype(F32)
    d_lat_keys = d_keys[:, :RANK]
    scale_lat = rms_scale(latent)
    latent_gain_g = jnp.sum(d_lat_keys * latent * scale_lat, axis=0)
    d_latent = norm_back(latent, scale_lat, lat_gain, d_lat_keys)
    first = d_keys[:, RANK : RANK + ROPE // 2]
    second = d_keys[:, RANK + ROPE // 2 : RANK + ROPE]
    cosine, sine = cosine[:, : ROPE // 2], sine[:, : ROPE // 2]
    d_latent_pre = jnp.concatenate(
        [
            d_latent,
            first * cosine + second * sine,
            second * cosine - first * sine,
            jnp.zeros((tokens, 128 - ROPE), F32),
        ],
        -1,
    ).astype(BF)
    input_grad, packed_b = one_step(
        functools.partial(last_kernel, rows, count),
        "last_norm",
        [
            hidden_rows,
            low_one,
            d_query_sum.reshape(tokens, width),
            d_latent_pre,
            d_middle.reshape(tokens, width),
        ]
        + blocks,
        [((tokens, width), F32), ((count, down_cols + 16, piece), BF)],
        [pltpu.VMEM((tokens, width), F32)],
        4 * tokens * width * (RANK + 128),
    )
    packed_b, d_query_pre = lax.optimization_barrier((packed_b, d_query_pre))
    input_grad = input_grad.reshape(seq_dev, block, width)
    packed_b = relayed(packed_b)
    gain_rows = by_shift(latent_gain_g.astype(BF).reshape(plane, rank_local))
    packed_b = packed_b.at[:, down_cols + 1, :rank_local].set(gain_rows)
    own_b = plane_reduce(packed_b, folds, chips_x)
    down_s = own_b[:down_cols].T
    attn_gain_s = own_b[down_cols]
    lat_gain_s = own_b[down_cols + 1, :rank_local]

    grads_a = one_step(
        functools.partial(attend_grads_kernel, rows, count, piece),
        "attend_grads",
        [attended, d_branch, d_query_pre, low_one],
        [((count, rows.query, piece), BF)],
        [],
        2 * tokens * width * rows.query,
    )[0]
    small_a = jnp.concatenate(
        [
            latent_up_g.astype(BF).reshape(plane, up_rows, rows_local),
            ffn_gain_g.astype(BF).reshape(plane, 1, rows_local),
            jnp.zeros((plane, 15, rows_local), BF),
        ],
        1,
    )
    packed_a = jnp.concatenate([relayed(grads_a), by_shift(small_a)], 1)
    own_a = plane_reduce(packed_a, folds, chips_x)
    query_own = own_a[rows.out : rows.query]
    rope_own = query_own[heads_dev * NOPE :].reshape(2, heads_dev, ROPE // 2, rows_local)
    query_s = jnp.concatenate(
        [
            query_own[: heads_dev * NOPE].reshape(heads_dev, NOPE, rows_local),
            rope_own.transpose(1, 0, 2, 3).reshape(heads_dev, ROPE, rows_local),
        ],
        1,
    ).reshape(query_cols, rows_local)
    query_s = query_s.T
    output_s = own_a[: rows.out]
    up_s = own_a[rows.query : rows.query + up_rows].reshape(rank_local, -1)
    ffn_gain_s = own_a[rows.query + up_rows]

    gate_up_grad = ffn_home[:, : sizes.row_a].reshape(EXPERTS, 2, units, rows_local)
    gate_up_grad = gate_up_grad.transpose(3, 0, 1, 2)
    down_grad = ffn_home[:, sizes.row_a : sizes.row_b].reshape(EXPERTS, units, rows_local)
    down_grad = down_grad.transpose(2, 0, 1)
    shared_gu_s = (
        ffn_home[:, sizes.row_b : sizes.row_c]
        .reshape(chips, 2, sizes.part, rows_local)[:, :, :shared_part]
        .transpose(3, 1, 0, 2)
        .reshape(rows_local, 2, shared_units)
    )
    shared_down_s = ffn_home[:, sizes.row_c :][:, :shared_part].reshape(shared_units, rows_local)
    moe_sum, gate_up_grad, down_grad = lax.optimization_barrier((moe_sum, gate_up_grad, down_grad))
    block_out = (middle + moe_sum.astype(F32)).astype(BF)
    return (
        block_out,
        input_grad,
        attn_gain_s,
        query_s,
        down_s,
        lat_gain_s,
        up_s,
        output_s,
        ffn_gain_s,
        shared_gu_s,
        shared_down_s,
        gate_up_grad,
        down_grad,
    )


def solution(mesh):
    placed = (
        P("fsdp", "ctx", None),
        P("fsdp"),
        P("fsdp", "ctx", None),
        P("fsdp", "ctx", None),
        P("fsdp", "ctx", None),
        P(("fsdp", "ctx")),
        P(("fsdp", "ctx"), "tp"),
        P(("fsdp", "ctx"), None),
        P(("fsdp", "ctx")),
        P(("fsdp", "ctx"), "tp"),
        P("tp", ("fsdp", "ctx")),
        P(("fsdp", "ctx")),
        P(("fsdp", "ctx"), None, "tp"),
        P("tp", ("fsdp", "ctx")),
        P(("fsdp", "ctx"), None, None, "tp"),
        P(("fsdp", "ctx"), None, "tp"),
    )
    return jax.shard_map(
        local,
        mesh=mesh,
        in_specs=placed,
        out_specs=(
            P("fsdp", "ctx", None),
            P("fsdp", "ctx", None),
            P(("fsdp", "ctx")),
            P(("fsdp", "ctx"), "tp"),
            P(("fsdp", "ctx"), None),
            P(("fsdp", "ctx")),
            P(("fsdp", "ctx"), "tp"),
            P("tp", ("fsdp", "ctx")),
            P(("fsdp", "ctx")),
            P(("fsdp", "ctx"), None, "tp"),
            P("tp", ("fsdp", "ctx")),
            P(("fsdp", "ctx"), None, None, "tp"),
            P(("fsdp", "ctx"), None, "tp"),
        ),
        check_vma=False,
    )
```

time: 2030 us -> 910 us (0.45)
  waiting for transfers between devices: 827 us -> 434 us
  local copies, waits for them, and re-layouts: 458 us -> 88.5 us
  blocking collectives: 303 us -> 0 us
  Pallas kernels: 0 us -> 237 us
  matrix products: 216 us -> 0.17 us
  other arithmetic: 138 us -> 81.6 us
    all_to_all x8 -> x1, waiting for transfers between devices: 323 us -> 0.01 us  [local(): lax.all_to_all(ffn_sum, PLANE, split_axis=0, concat_axis=0, axis_index_gr...]
    ppermute x0 -> x42, waiting for transfers between devices: none -> 286 us  [the longest x29 278 us: chip_shift(): return lax.ppermute(value, PLANE, pairs)]
    all_gather x3 -> x0, blocking collectives: 278 us -> none  [the longest x1 191 us: local(): lax.all_gather(rope_low, 'ctx', axis=1, tiled=True)]
    pallas_call x0 -> x10, Pallas kernels: none -> 237 us  [the longest x4 121 us: chunk_call(): pl.pallas_call(functools.partial(chunk_kernel, sizes, straight), grid=(1,...]
    dot_general x33 -> x1, matrix products: 216 us -> 0.17 us  [dot(): return jnp.einsum(spec, a, b, preferred_element_type=F32)]
    convert_element_type x8 -> x5, local copies, waits for them, and re-layouts: 153 us -> 0.89 us  [the longest x2 0.73 us: local(): lat_gain = gain_all[:, 2, :rank_local].reshape(RANK).astype(F32)]
    psum x3 -> x4, waiting for transfers between devices: 287 us -> 147 us  [the longest x1 84.7 us: local(): d_keys, d_query_sum = lax.psum((d_keys_ctx, d_query_in), 'tp')]
    gather x4, local copies, waits for them, and re-layouts: 124 us -> 2.38 us  [the longest x2 1.19 us: in_order(): return jnp.take(jnp.stack(parts), order, axis=0)]
  transfers between devices with their start and end apart: 26 -> 47, of which waited for: 13 -> 23; matrix products, arithmetic and copies ran while one was open for 33% -> 16% of each run, Pallas kernels for 0% -> 26%
where the time goes in v1:
time: 910 us; the launch traced here: 901 us
  waiting for transfers between devices  434 us (48%)
  Pallas kernels  237 us (26%)
  local copies, waits for them, and re-layouts  88.5 us (10%)
  other arithmetic  81.6 us (9%)
  starting transfers between devices  45.1 us (5%)
  between operations  14.9 us (2%)
    ppermute x29, waiting for transfers between devices, chip_shift(): return lax.ppermute(value, PLANE, pairs)  278 us
    pallas_call x4, Pallas kernels, chunk_call(): pl.pallas_call(functools.partial(chunk_kernel, sizes, straight), grid=(1,...  121 us
    psum x1, waiting for transfers between devices, local(): d_keys, d_query_sum = lax.psum((d_keys_ctx, d_query_in), 'tp')  84.7 us
    pallas_call x5, Pallas kernels, one_step(): pl.pallas_call(body, grid=(1,), in_specs=smem + specs, out_specs=[whole_s...  75.6 us
    psum x1, waiting for transfers between devices, local(): attn_sum = lax.psum(attn_part, 'tp')  55.3 us
    pallas_call x1, Pallas kernels, weight_grad_call(): pl.pallas_call(functools.partial(weight_grad_kernel, sizes, straight), gr...  41 us
    ppermute x29, starting transfers between devices, chip_shift(): return lax.ppermute(value, PLANE, pairs)  36.4 us
    unnamed x75, local copies, waits for them, and re-layouts  26.7 us
  transfers between devices with their start and end apart: 47, of which 23 were waited for; matrix products, arithmetic and copies ran while one was open for 16% of the time, Pallas kernels for 26%

profile of v1, /device:TPU:0, one launch (start us, length us, event | category | flops | bytes accessed | tf_op | source)
XLA Modules:
  0.0 901.1 jit_solution(12335657410296060454)
XLA Ops:
  17.2 3.0 collective-permute-start.1
  23.9 2.0 copy.72
  26.7 1.8 fusion.7
  28.5 10.0 %pad_maximum_fusion = bf16[4,4752,256]{2,1,0:T(8,128)(2,1)S(1)} fusion(bf16[4,176,256]{2,1,0:T(8,128)(2,1)} %bitcast.279, bf16[4,352,256]{2,1,0:T(8,128)(2,1)} %bitcast.255, bf16[4,1408,256]{2,1,0:T(8,128)(2,1)} %bitcast.256, bf16[4,2816,256]{2,1,0:T(8,128)(2,1)} %bitcast.251), kind=kLoop, calls=%fused_computation.5 | loop fusion | flops 38928384 | bytes 19464192 | tf_op jit(solution)/shard_map/concatenate | solution.py:722
  38.5 7.3 collective-permute-done.1.refs_2_
  45.9 1.6 collective-permute-done.refs_1_
  51.3 3.9 dynamic-slice_bitcast_fusion
  55.9 9.7 %collective-permute-done.2 = bf16[2256,128]{1,0:T(8,128)(2,1)} collective-permute-done((bf16[2256,128]{1,0:T(8,128)(2,1)S(1)}, bf16[2256,128]{1,0:T(8,128)(2,1)}, u32[]{:S(2)}, u32[]{:S(2)}) %collective-permute-start.2) | collective-permute-done | bytes 577568 | tf_op jit(solution)/shard_map/ppermute | solution.py:70
  75.9 10.7 %project.1 = (bf16[512,2048]{1,0:T(8,128)(2,1)}, bf16[512,512]{1,0:T(8,128)(2,1)}, bf16[512,256]{1,0:T(8,128)(2,1)}, bf16[512,640]{1,0:T(8,128)(2,1)}, f32[512,512]{1,0:T(8,128)}) custom-call(bf16[512,2048]{1,0:T(8,128)(2,1)} %bitcast.243, f32[1,512]{1,0:T(1,128)} %reshape.1144.gain_ref, f32[512,128]{1,0:T(8,128)} %copy.73.cos_ref, ...), custom_call_target="tpu_custom_call" | custom-call | flops 3221225472 | bytes 8388608 | tf_op jit(solution)/shard_map/project/pallas_call | solution.py:495
  90.8 50.0 %collective-permute-done.8 = bf16[2,256,640]{2,1,0:T(8,128)(2,1)S(1)} collective-permute-done((bf16[2,256,640]{2,1,0:T(8,128)(2,1)}, bf16[2,256,640]{2,1,0:T(8,128)(2,1)S(1)}, u32[]{:S(2)}, u32[]{:S(2)}) %collective-permute-start.8) | collective-permute-done | bytes 655392 | tf_op jit(solution)/shard_map/ppermute | solution.py:70
  140.8 2.3 pad_maximum_fusion.3
  148.4 1.9 select_n.265.up_ref
  150.4 3.1 pad_maximum_fusion.2.keys_ref
  153.5 11.0 %collective-permute-done.11.refs_6_ = bf16[4752,256]{1,0:T(8,128)(2,1)} collective-permute-done((bf16[4752,256]{1,0:T(8,128)(2,1)}, bf16[4752,256]{1,0:T(8,128)(2,1)}, u32[]{:S(2)}, u32[]{:S(2)}) %collective-permute-start.11) | collective-permute-done | bytes 2433056 | tf_op jit(solution)/shard_map/ppermute | solution.py:70
  166.5 15.2 %attend.1 = (bf16[512,2048]{1,0:T(8,128)(2,1)}, bf16[512,512]{1,0:T(8,128)(2,1)}, bf16[2,1024,1024]{2,1,0:T(8,128)(2,1)}, f32[512,128]{1,0:T(8,128)}) custom-call(s32[2]{0:T(128)} %lengths_ref.3, bf16[512,512]{1,0:T(8,128)(2,1)} %get-tuple-element.115.nope_ref, bf16[512,256]{1,0:T(8,128)(2,1)} %get-tuple-element.116.rope_ref, ...), custom_call_target="tpu_custom_call" | custom-call | flops 3758096384 | bytes 8388608 | tf_op jit(solution)/shard_map/attend/pallas_call | solution.py:495
  182.6 30.7 %collective-permute-done.13.refs_3_.refs_9_ = bf16[512,2048]{1,0:T(8,128)(2,1)} collective-permute-done((bf16[512,2048]{1,0:T(8,128)(2,1)}, bf16[512,2048]{1,0:T(8,128)(2,1)}, u32[]{:S(2)}, u32[]{:S(2)}) %collective-permute-start.13) | collective-permute-done | bytes 2097184 | tf_op jit(solution)/shard_map/ppermute | solution.py:70
  213.4 55.3 %all-reduce.9.cloned.1.call-done = bf16[2,256,2048]{2,1,0:T(8,128)(2,1)} async-done(((bf16[2,256,2048]{2,1,0:T(8,128)(2,1)}), bf16[2,256,2048]{2,1,0:T(8,128)(2,1)}) %all-reduce.9.cloned.1.call-update) | async-done | bytes 2097168 | tf_op jit(solution)/shard_map/psum | solution.py:860
  272.4 2.5 multiply_reduce_fusion
  274.9 2.4 multiply_convert_fusion
  282.3 30.0 %expert_rows.4 = (bf16[512,2048]{1,0:T(8,128)(2,1)}, bf16[512,2048]{1,0:T(8,128)(2,1)}, bf16[4224,1024]{1,0:T(8,128)(2,1)}, bf16[528,2048]{1,0:T(8,128)(2,1)}) custom-call(f32[8,512]{1,0:T(8,128)} %get-tuple-element.248.refs_0_, f32[8,512]{1,0:T(8,128)} %get-tuple-element.244.refs_1_, bf16[512,2048]{1,0:T(8,128)(2,1)} %bitcast.68.refs_2_.refs_4_, ...), custom_call_target="tpu_custom_call" | custom-call | flops 15367929856 | bytes 19464192 | tf_op jit(solution)/shard_map/expert_rows/pallas_call | solution.py:276
  312.3 13.3 %collective-permute-done.20.refs_2_.refs_6_ = bf16[512,2048]{1,0:T(8,128)(2,1)} collective-permute-done((bf16[512,2048]{1,0:T(8,128)(2,1)}, bf16[512,2048]{1,0:T(8,128)(2,1)}, u32[]{:S(2)}, u32[]{:S(2)}) %collective-permute-start.20) | collective-permute-done | bytes 2097184 | tf_op jit(solution)/shard_map/ppermute | solution.py:70
  326.9 2.3 slice.304
  329.1 2.3 slice.306
  332.7 2.3 slice.307
  339.0 30.5 %expert_rows.5 = (bf16[512,2048]{1,0:T(8,128)(2,1)}, bf16[512,2048]{1,0:T(8,128)(2,1)}, bf16[4224,1024]{1,0:T(8,128)(2,1)}, bf16[528,2048]{1,0:T(8,128)(2,1)}) custom-call(f32[8,512]{1,0:T(8,128)} %get-tuple-element.247.refs_0_, f32[8,512]{1,0:T(8,128)} %get-tuple-element.243.refs_1_, ...), custom_call_target="tpu_custom_call", output_to_operand_aliasing={{2}: (12, {}), {3}: (13, {})} | custom-call | flops 15367929856 | bytes 19464192 | tf_op jit(solution)/shard_map/expert_rows/pallas_call | solution.py:276
  369.6 1.5 collective-permute-start.21
  371.1 30.0 %expert_rows.6 = (bf16[512,2048]{1,0:T(8,128)(2,1)}, bf16[512,2048]{1,0:T(8,128)(2,1)}, bf16[4224,1024]{1,0:T(8,128)(2,1)}, bf16[528,2048]{1,0:T(8,128)(2,1)}) custom-call(f32[8,512]{1,0:T(8,128)} %get-tuple-element.246.refs_0_, f32[8,512]{1,0:T(8,128)} %get-tuple-element.242.refs_1_, ...), custom_call_target="tpu_custom_call", output_to_operand_aliasing={{2}: (12, {}), {3}: (13, {})} | custom-call | flops 15367929856 | bytes 19464192 | tf_op jit(solution)/shard_map/expert_rows/pallas_call | solution.py:276
  403.1 2.4 constant_dynamic-update-slice_fusion.17
  408.1 2.3 constant_dynamic-update-slice_fusion.16.refs_2_.refs_7_
  410.4 30.0 %expert_rows.7 = (bf16[512,2048]{1,0:T(8,128)(2,1)}, bf16[512,2048]{1,0:T(8,128)(2,1)}, bf16[4224,1024]{1,0:T(8,128)(2,1)}, bf16[528,2048]{1,0:T(8,128)(2,1)}) custom-call(f32[8,512]{1,0:T(8,128)} %get-tuple-element.245.refs_0_, f32[8,512]{1,0:T(8,128)} %get-tuple-element.241.refs_1_, ...), custom_call_target="tpu_custom_call", output_to_operand_aliasing={{2}: (12, {}), {3}: (13, {})} | custom-call | flops 15367929856 | bytes 19464192 | tf_op jit(solution)/shard_map/expert_rows/pallas_call | solution.py:276
  442.0 41.0 %expert_weight_grads.1 = (bf16[4,4752,256]{2,1,0:T(8,128)(2,1)}, bf16[4,4752,256]{2,1,0:T(8,128)(2,1)}) custom-call(f32[4,8,512]{2,1,0:T(8,128)} %get-tuple-element.239.refs_0_, f32[4,8,512]{2,1,0:T(8,128)} %bitcast.280, bf16[4224,1024]{1,0:T(8,128)(2,1)} %get-tuple-element.143.refs_2_, bf16[528,2048]{1,0:T(8,128)(2,1)} %get-tuple-element.144.refs_3_, ...), custom_call_target="tpu_custom_call" | custom-call | flops 30735859712 | bytes 38928384 | tf_op jit(solution)/shard_map/expert_weight_grads/pallas_call | solution.py:380
  483.0 9.0 collective-permute-done.22
  492.0 6.8 add_convert_fusion.4
  499.9 2.3 collective-permute-start.30
  502.7 44.8 %collective-permute-done.28 = bf16[512,2048]{1,0:T(8,128)(2,1)} collective-permute-done((bf16[512,2048]{1,0:T(8,128)(2,1)}, bf16[512,2048]{1,0:T(8,128)(2,1)}, u32[]{:S(2)}, u32[]{:S(2)}) %collective-permute-start.28) | collective-permute-done | bytes 2097184 | tf_op jit(solution)/shard_map/ppermute | solution.py:70
  547.5 44.8 %collective-permute-done.29 = bf16[512,2048]{1,0:T(8,128)(2,1)} collective-permute-done((bf16[512,2048]{1,0:T(8,128)(2,1)}, bf16[512,2048]{1,0:T(8,128)(2,1)}, u32[]{:S(2)}, u32[]{:S(2)}) %collective-permute-start.29) | collective-permute-done | bytes 2097184 | tf_op jit(solution)/shard_map/ppermute | solution.py:70
  592.3 6.8 add_convert_fusion.3
  599.1 4.0 fusion.6
  603.3 3.9 fusion.40
  607.2 27.1 %attend_back.1 = (bf16[512,768]{1,0:T(8,128)(2,1)}, bf16[512,2048]{1,0:T(8,128)(2,1)}, bf16[4,2,256,640]{3,2,1,0:T(8,128)(2,1)}, f32[512,1024]{1,0:T(8,128)}) custom-call(s32[2]{0:T(128)} %lengths_ref.3, bf16[512,2048]{1,0:T(8,128)(2,1)} %bitcast.249, bf16[512,512]{1,0:T(8,128)(2,1)} %get-tuple-element.115.nope_ref, ...), custom_call_target="tpu_custom_call" | custom-call | flops 7516192768 | bytes 8388608 | tf_op jit(solution)/shard_map/attend_back/pallas_call | solution.py:495
  634.3 2.6 slice.310
  637.0 3.3 collective-permute-done.31
  640.3 1.6 convert_add_fusion.1
  645.4 15.0 %collective-permute-done.32 = bf16[2,256,640]{2,1,0:T(8,128)(2,1)S(1)} collective-permute-done((bf16[2,256,640]{2,1,0:T(8,128)(2,1)S(1)}, bf16[2,256,640]{2,1,0:T(8,128)(2,1)S(1)}, u32[]{:S(2)}, u32[]{:S(2)}) %collective-permute-start.32) | collective-permute-done | bytes 655392 | tf_op jit(solution)/shard_map/ppermute | solution.py:70
  660.3 2.3 fusion.12
  662.8 1.7 convert_element_type.272
  666.3 12.3 %add_convert_fusion = bf16[4,4752,256]{2,1,0:T(8,128)(2,1)} fusion(bf16[4,4752,256]{2,1,0:T(8,128)(2,1)} %collective-permute-done.33, bf16[4,4752,256]{2,1,0:T(8,128)(2,1)} %get-tuple-element.173), kind=kLoop, calls=%fused_computation.4 | loop fusion | flops 19464192 | bytes 29196288 | tf_op jit(solution)/shard_map/convert_element_type | solution.py:965
  678.6 5.9 all-to-all-start
  684.8 84.7 %all-reduce.15.cloned.1.call-done = (bf16[2,256,640]{2,1,0:T(8,128)(2,1)}, bf16[512,2048]{1,0:T(8,128)(2,1)}) async-done(((bf16[2,256,640]{2,1,0:T(8,128)(2,1)}, bf16[512,2048]{1,0:T(8,128)(2,1)}), (bf16[2,256,640]{2,1,0:T(8,128)(2,1)}, bf16[512,2048]{1,0:T(8,128)(2,1)})) %all-reduce.15.cloned.1.call-update) | async-done | bytes 2752528 | tf_op jit(solution)/shard_map/psum | solution.py:964
  772.6 14.7 %last_norm.1 = (f32[512,2048]{1,0:T(8,128)}, bf16[8,592,256]{2,1,0:T(8,128)(2,1)}) custom-call(bf16[512,2048]{1,0:T(8,128)(2,1)} %bitcast.244, bf16[512,2048]{1,0:T(8,128)(2,1)} %get-tuple-element.176.low_ref, bf16[512,2048]{1,0:T(8,128)(2,1)} %get-tuple-element.177.dq_ref, bf16[512,640]{1,0:T(8,128)(2,1)} %maximum_maximum_fusion.1.dlat_ref, ...), custom_call_target="tpu_custom_call" | custom-call | flops 2684354560 | bytes 8388608 | tf_op jit(solution)/shard_map/last_norm/pallas_call | solution.py:495
  787.3 8.0 attend_grads.1
  795.2 3.7 pad_maximum_fusion.1
  801.9 4.9 collective-permute-done.34
  806.7 1.6 add_convert_fusion.5
  812.0 2.3 add_convert_fusion.1
  820.0 6.0 collective-permute-done.37
  826.0 1.9 collective-permute-done.36
  830.0 12.1 %collective-permute-done.39 = bf16[1552,256]{1,0:T(8,128)(2,1)S(1)} collective-permute-done((bf16[1552,256]{1,0:T(8,128)(2,1)S(1)}, bf16[1552,256]{1,0:T(8,128)(2,1)S(1)}, u32[]{:S(2)}, u32[]{:S(2)}) %collective-permute-start.39) | collective-permute-done | bytes 794656 | tf_op jit(solution)/shard_map/ppermute | solution.py:70
  842.1 17.3 %collective-permute-done.41 = bf16[1552,256]{1,0:T(8,128)(2,1)S(1)} collective-permute-done((bf16[1552,256]{1,0:T(8,128)(2,1)S(1)}, bf16[1552,256]{1,0:T(8,128)(2,1)S(1)}, u32[]{:S(2)}, u32[]{:S(2)}) %collective-permute-start.41) | collective-permute-done | bytes 794656 | tf_op jit(solution)/shard_map/ppermute | solution.py:70
  867.0 4.9 slice.376
  871.9 8.2 slice.375
  880.1 7.4 all-reduce.13.cloned.1.call-done
  887.5 4.8 add_convert_fusion.2
  892.4 1.9 slice.403
  (255 shorter events, 95.4 us)
Async XLA Ops:
  7.2 5.1 copy-start.22
  7.2 5.3 copy-start.20
  7.2 7.4 copy-start.19
  7.2 261.4 %all-reduce.9.cloned.1.call-start = ((), (), s32[]{:S(2)}) async-start(), calls=%async_computation.1 | async-start | bytes 4194304 | tf_op jit(solution)/shard_map/psum | solution.py:860
  17.2 28.6 %collective-permute-start.1 = (bf16[2256,256]{1,0:T(8,128)(2,1)}, bf16[2256,256]{1,0:T(8,128)(2,1)S(1)}, u32[]{:S(2)}, u32[]{:S(2)}) collective-permute-start(bf16[2256,256]{1,0:T(8,128)(2,1)} %constant_dynamic-update-slice_fusion.refs_0_), channel_id=1, source_target_pairs={{0,16},{4,20},{8,24},{12,28},{16,0},{20,4},{24,8},{28,12},{1,17},{... | collective-permute-start | bytes 3465224 | tf_op jit(solution)/shard_map/ppermute | solution.py:70
  20.2 27.2 %collective-permute-start = (bf16[2256,256]{1,0:T(8,128)(2,1)}, bf16[2256,256]{1,0:T(8,128)(2,1)}, u32[]{:S(2)}, u32[]{:S(2)}) collective-permute-start(bf16[2256,256]{1,0:T(8,128)(2,1)} %constant_dynamic-update-slice_fusion.refs_0_), channel_id=1, source_target_pairs={{0,8},{4,12},{8,0},{12,4},{16,24},{20,28},{24,16},{28,20},{1,9},{5... | collective-permute-start | bytes 3465224 | tf_op jit(solution)/shard_map/ppermute | solution.py:70
  21.8 4.8 copy-start.7
  45.9 23.5 %copy-start.10 = (bf16[2256,256]{1,0:T(8,128)(2,1)}, bf16[2256,256]{1,0:T(8,128)(2,1)S(1)}, u32[]{:S(2)}) copy-start(bf16[2256,256]{1,0:T(8,128)(2,1)S(1)} %collective-permute-done.1.refs_2_) | copy-start | bytes 3465220
  48.5 23.0 %collective-permute-start.5 = (bf16[2256,256]{1,0:T(8,128)(2,1)}, bf16[2256,256]{1,0:T(8,128)(2,1)}, u32[]{:S(2)}, u32[]{:S(2)}) collective-permute-start(bf16[2256,256]{1,0:T(8,128)(2,1)} %collective-permute-done.refs_1_), channel_id=1, source_target_pairs={{0,4},{4,0},{8,12},{12,8},{16,20},{20,16},{24,28},{28,24},{1,5},{5... | collective-permute-start | bytes 3465224 | tf_op jit(solution)/shard_map/ppermute | solution.py:75
  48.7 24.1 %collective-permute-start.6 = (bf16[2256,256]{1,0:T(8,128)(2,1)S(1)}, bf16[2256,256]{1,0:T(8,128)(2,1)}, u32[]{:S(2)}, u32[]{:S(2)}) collective-permute-start(bf16[2256,256]{1,0:T(8,128)(2,1)S(1)} %collective-permute-done.1.refs_2_), channel_id=1, source_target_pairs={{0,4},{4,0},{8,12},{12,8},{16,20},{20,16},{24,28},{28,24},{1,5},{5... | collective-permute-start | bytes 3465224 | tf_op jit(solution)/shard_map/ppermute | solution.py:75
  49.2 18.1 %collective-permute-start.3 = (bf16[2256,128]{1,0:T(8,128)(2,1)S(1)}, bf16[2256,128]{1,0:T(8,128)(2,1)}, u32[]{:S(2)}, u32[]{:S(2)}) collective-permute-start(bf16[2256,128]{1,0:T(8,128)(2,1)S(1)} %slice.273), channel_id=1, source_target_pairs={{0,8},{4,12},{8,0},{12,4},{16,24},{20,28},{24,16},{28,20},{1,9},{5... | collective-permute-start | bytes 1732616 | tf_op jit(solution)/shard_map/ppermute | solution.py:70
  50.7 14.9 %collective-permute-start.2 = (bf16[2256,128]{1,0:T(8,128)(2,1)S(1)}, bf16[2256,128]{1,0:T(8,128)(2,1)}, u32[]{:S(2)}, u32[]{:S(2)}) collective-permute-start(bf16[2256,128]{1,0:T(8,128)(2,1)S(1)} %slice.272), channel_id=1, source_target_pairs={{0,16},{4,20},{8,24},{12,28},{16,0},{20,4},{24,8},{28,12},{1,17},{... | collective-permute-start | bytes 1732616 | tf_op jit(solution)/shard_map/ppermute | solution.py:70
  51.3 18.1 %collective-permute-start.4 = (bf16[2256,256]{1,0:T(8,128)(2,1)}, bf16[2256,256]{1,0:T(8,128)(2,1)}, u32[]{:S(2)}, u32[]{:S(2)}) collective-permute-start(bf16[2256,256]{1,0:T(8,128)(2,1)} %constant_dynamic-update-slice_fusion.refs_0_), channel_id=1, source_target_pairs={{0,4},{4,0},{8,12},{12,8},{16,20},{20,16},{24,28},{28,24},{1,5},{5... | collective-permute-start | bytes 3465224 | tf_op jit(solution)/shard_map/ppermute | solution.py:75
  65.6 117.0 %collective-permute-start.14 = (bf16[512,2048]{1,0:T(8,128)(2,1)}, bf16[512,2048]{1,0:T(8,128)(2,1)}, u32[]{:S(2)}, u32[]{:S(2)}) collective-permute-start(bf16[512,2048]{1,0:T(8,128)(2,1)} %bitcast.22.refs_3_.refs_8_), channel_id=1, source_target_pairs={{0,16},{4,20},{8,24},{12,28},{16,0},{20,4},{24,8},{28,12},{1,17},{... | collective-permute-start | bytes 6291464 | tf_op jit(solution)/shard_map/ppermute | solution.py:70
  68.5 7.3 copy-start.11
  68.5 4.9 collective-permute-start.7
  69.4 95.1 %collective-permute-start.11 = (bf16[4752,256]{1,0:T(8,128)(2,1)}, bf16[4752,256]{1,0:T(8,128)(2,1)}, u32[]{:S(2)}, u32[]{:S(2)}) collective-permute-start(bf16[4752,256]{1,0:T(8,128)(2,1)} %get-tuple-element.223), channel_id=1, source_target_pairs={{0,16},{4,20},{8,24},{12,28},{16,0},{20,4},{24,8},{28,12},{1,17},{... | collective-permute-start | bytes 7299080 | tf_op jit(solution)/shard_map/ppermute | solution.py:70
  71.6 92.9 %collective-permute-start.10 = (bf16[4752,256]{1,0:T(8,128)(2,1)}, bf16[4752,256]{1,0:T(8,128)(2,1)}, u32[]{:S(2)}, u32[]{:S(2)}) collective-permute-start(bf16[4752,256]{1,0:T(8,128)(2,1)} %get-tuple-element.224), channel_id=1, source_target_pairs={{0,8},{4,12},{8,0},{12,4},{16,24},{20,28},{24,16},{28,20},{1,9},{5... | collective-permute-start | bytes 7299080 | tf_op jit(solution)/shard_map/ppermute | solution.py:70
  86.5 54.2 %collective-permute-start.8 = (bf16[2,256,640]{2,1,0:T(8,128)(2,1)}, bf16[2,256,640]{2,1,0:T(8,128)(2,1)S(1)}, u32[]{:S(2)}, u32[]{:S(2)}) collective-permute-start(bf16[2,256,640]{2,1,0:T(8,128)(2,1)} %bitcast.257), channel_id=1, source_target_pairs={{0,8},{4,12},{8,0},{12,4},{16,24},{20,28},{24,16},{28,20},{1,9},{5... | collective-permute-start | bytes 1966088 | tf_op jit(solution)/shard_map/ppermute | solution.py:70
  143.0 7.3 collective-permute-start.9
  164.5 48.9 %collective-permute-start.13 = (bf16[512,2048]{1,0:T(8,128)(2,1)}, bf16[512,2048]{1,0:T(8,128)(2,1)}, u32[]{:S(2)}, u32[]{:S(2)}) collective-permute-start(bf16[512,2048]{1,0:T(8,128)(2,1)} %bitcast.22.refs_3_.refs_8_), channel_id=1, source_target_pairs={{0,8},{4,12},{8,0},{12,4},{16,24},{20,28},{24,16},{28,20},{1,9},{5... | collective-permute-start | bytes 6291464 | tf_op jit(solution)/shard_map/ppermute | solution.py:70
  165.0 103.6 %collective-permute-start.12 = (bf16[4752,256]{1,0:T(8,128)(2,1)}, bf16[4752,256]{1,0:T(8,128)(2,1)}, u32[]{:S(2)}, u32[]{:S(2)}) collective-permute-start(bf16[4752,256]{1,0:T(8,128)(2,1)} %get-tuple-element.113), channel_id=1, source_target_pairs={{0,24},{4,28},{8,16},{12,20},{16,8},{20,12},{24,0},{28,4},{1,25},{... | collective-permute-start | bytes 7299080 | tf_op jit(solution)/shard_map/ppermute | solution.py:70
  181.7 90.7 %copy-start = (bf16[2,256,2048]{2,1,0:T(8,128)(2,1)S(1)}, bf16[2,256,2048]{2,1,0:T(8,128)(2,1)}, u32[]{:S(2)}) copy-start(bf16[2,256,2048]{2,1,0:T(8,128)(2,1)} %param.18) | copy-start | bytes 6291460
  181.7 417.4 %all-reduce.11.cloned.1.call-start = ((), (), s32[]{:S(2)}) async-start(), calls=%async_computation.2 | async-start | bytes 4194304 | tf_op jit(solution)/shard_map/psum | solution.py:922
  182.0 96.8 %collective-permute-start.15 = (bf16[4752,256]{1,0:T(8,128)(2,1)}, bf16[4752,256]{1,0:T(8,128)(2,1)}, u32[]{:S(2)}, u32[]{:S(2)}) collective-permute-start(bf16[4752,256]{1,0:T(8,128)(2,1)} %get-tuple-element.121.refs_4_), channel_id=1, source_target_pairs={{0,4},{4,0},{8,12},{12,8},{16,20},{20,16},{24,28},{28,24},{1,5},{5... | collective-permute-start | bytes 7299080 | tf_op jit(solution)/shard_map/ppermute | solution.py:75
  182.0 100.2 %collective-permute-start.16 = (bf16[4752,256]{1,0:T(8,128)(2,1)}, bf16[4752,256]{1,0:T(8,128)(2,1)}, u32[]{:S(2)}, u32[]{:S(2)}) collective-permute-start(bf16[4752,256]{1,0:T(8,128)(2,1)} %collective-permute-done.10.refs_5_), channel_id=1, source_target_pairs={{0,4},{4,0},{8,12},{12,8},{16,20},{20,16},{24,28},{28,24},{1,5},{5... | collective-permute-start | bytes 7299080 | tf_op jit(solution)/shard_map/ppermute | solution.py:75
  182.5 99.7 %collective-permute-start.17 = (bf16[4752,256]{1,0:T(8,128)(2,1)}, bf16[4752,256]{1,0:T(8,128)(2,1)}, u32[]{:S(2)}, u32[]{:S(2)}) collective-permute-start(bf16[4752,256]{1,0:T(8,128)(2,1)} %collective-permute-done.11.refs_6_), channel_id=1, source_target_pairs={{0,4},{4,0},{8,12},{12,8},{16,20},{20,16},{24,28},{28,24},{1,5},{5... | collective-permute-start | bytes 7299080 | tf_op jit(solution)/shard_map/ppermute | solution.py:75
  268.7 13.6 %collective-permute-start.18 = (bf16[4752,256]{1,0:T(8,128)(2,1)}, bf16[4752,256]{1,0:T(8,128)(2,1)}, u32[]{:S(2)}, u32[]{:S(2)}) collective-permute-start(bf16[4752,256]{1,0:T(8,128)(2,1)} %collective-permute-done.12.refs_7_), channel_id=1, source_target_pairs={{0,4},{4,0},{8,12},{12,8},{16,20},{20,16},{24,28},{28,24},{1,5},{5... | collective-permute-start | bytes 7299080 | tf_op jit(solution)/shard_map/ppermute | solution.py:75
  277.3 48.4 %collective-permute-start.20 = (bf16[512,2048]{1,0:T(8,128)(2,1)}, bf16[512,2048]{1,0:T(8,128)(2,1)}, u32[]{:S(2)}, u32[]{:S(2)}) collective-permute-start(bf16[512,2048]{1,0:T(8,128)(2,1)} %bitcast.68.refs_2_.refs_4_), channel_id=1, source_target_pairs={{0,16},{4,20},{8,24},{12,28},{16,0},{20,4},{24,8},{28,12},{1,17},{... | collective-permute-start | bytes 6291464 | tf_op jit(solution)/shard_map/ppermute | solution.py:70
  278.8 48.1 %collective-permute-start.19 = (bf16[512,2048]{1,0:T(8,128)(2,1)}, bf16[512,2048]{1,0:T(8,128)(2,1)}, u32[]{:S(2)}, u32[]{:S(2)}) collective-permute-start(bf16[512,2048]{1,0:T(8,128)(2,1)} %bitcast.68.refs_2_.refs_4_), channel_id=1, source_target_pairs={{0,8},{4,12},{8,0},{12,4},{16,24},{20,28},{24,16},{28,20},{1,9},{5... | collective-permute-start | bytes 6291464 | tf_op jit(solution)/shard_map/ppermute | solution.py:70
  281.6 30.7 %copy-start.21 = (f32[4,8,1,512]{3,1,0,2:T(8,128)}, f32[4,8,1,512]{3,1,0,2:T(8,128)S(1)}, u32[]{:S(2)}) copy-start(f32[4,8,1,512]{3,1,0,2:T(8,128)S(1)} %get-tuple-element.240) | copy-start | bytes 196612
  335.0 70.5 %collective-permute-start.26 = (bf16[512,1024]{1,0:T(8,128)(2,1)}, bf16[512,1024]{1,0:T(8,128)(2,1)}, u32[]{:S(2)}, u32[]{:S(2)}) collective-permute-start(bf16[512,1024]{1,0:T(8,128)(2,1)} %slice.307), channel_id=1, source_target_pairs={{0,8},{4,12},{8,0},{12,4},{16,24},{20,28},{24,16},{28,20},{1,9},{5... | collective-permute-start | bytes 3145736 | tf_op jit(solution)/shard_map/ppermute | solution.py:70
  336.5 70.3 %collective-permute-start.24 = (bf16[512,1024]{1,0:T(8,128)(2,1)S(1)}, bf16[512,1024]{1,0:T(8,128)(2,1)}, u32[]{:S(2)}, u32[]{:S(2)}) collective-permute-start(bf16[512,1024]{1,0:T(8,128)(2,1)S(1)} %slice.305), channel_id=1, source_target_pairs={{0,8},{4,12},{8,0},{12,4},{16,24},{20,28},{24,16},{28,20},{1,9},{5... | collective-permute-start | bytes 3145736 | tf_op jit(solution)/shard_map/ppermute | solution.py:70
  337.0 64.1 %collective-permute-start.25 = (bf16[512,1024]{1,0:T(8,128)(2,1)}, bf16[512,1024]{1,0:T(8,128)(2,1)}, u32[]{:S(2)}, u32[]{:S(2)}) collective-permute-start(bf16[512,1024]{1,0:T(8,128)(2,1)} %slice.306), channel_id=1, source_target_pairs={{0,16},{4,20},{8,24},{12,28},{16,0},{20,4},{24,8},{28,12},{1,17},{... | collective-permute-start | bytes 3145736 | tf_op jit(solution)/shard_map/ppermute | solution.py:70
  337.6 65.5 %collective-permute-start.23 = (bf16[512,1024]{1,0:T(8,128)(2,1)}, bf16[512,1024]{1,0:T(8,128)(2,1)}, u32[]{:S(2)}, u32[]{:S(2)}) collective-permute-start(bf16[512,1024]{1,0:T(8,128)(2,1)} %slice.304), channel_id=1, source_target_pairs={{0,16},{4,20},{8,24},{12,28},{16,0},{20,4},{24,8},{28,12},{1,17},{... | collective-permute-start | bytes 3145736 | tf_op jit(solution)/shard_map/ppermute | solution.py:70
  369.6 113.5 %collective-permute-start.21 = (bf16[512,2048]{1,0:T(8,128)(2,1)}, bf16[512,2048]{1,0:T(8,128)(2,1)}, u32[]{:S(2)}, u32[]{:S(2)}) collective-permute-start(bf16[512,2048]{1,0:T(8,128)(2,1)} %get-tuple-element.134), channel_id=1, source_target_pairs={{0,8},{4,12},{8,0},{12,4},{16,24},{20,28},{24,16},{28,20},{1,9},{5... | collective-permute-start | bytes 6291464 | tf_op jit(solution)/shard_map/ppermute | solution.py:70
  401.1 90.9 %collective-permute-start.22 = (bf16[512,2048]{1,0:T(8,128)(2,1)}, bf16[512,2048]{1,0:T(8,128)(2,1)}, u32[]{:S(2)}, u32[]{:S(2)}) collective-permute-start(bf16[512,2048]{1,0:T(8,128)(2,1)} %get-tuple-element.139), channel_id=1, source_target_pairs={{0,16},{4,20},{8,24},{12,28},{16,0},{20,4},{24,8},{28,12},{1,17},{... | collective-permute-start | bytes 6291464 | tf_op jit(solution)/shard_map/ppermute | solution.py:70
  440.5 51.5 %collective-permute-start.27 = (bf16[512,2048]{1,0:T(8,128)(2,1)}, bf16[512,2048]{1,0:T(8,128)(2,1)}, u32[]{:S(2)}, u32[]{:S(2)}) collective-permute-start(bf16[512,2048]{1,0:T(8,128)(2,1)} %get-tuple-element.142), channel_id=1, source_target_pairs={{0,24},{4,28},{8,16},{12,20},{16,8},{20,12},{24,0},{28,4},{1,25},{... | collective-permute-start | bytes 6291464 | tf_op jit(solution)/shard_map/ppermute | solution.py:70
  492.0 170.6 %collective-permute-start.33 = (bf16[4,4752,256]{2,1,0:T(8,128)(2,1)}, bf16[4,4752,256]{2,1,0:T(8,128)(2,1)}, u32[]{:S(2)}, u32[]{:S(2)}) collective-permute-start(bf16[4,4752,256]{2,1,0:T(8,128)(2,1)} %get-tuple-element.167), channel_id=1, source_target_pairs={{0,4},{4,0},{8,12},{12,8},{16,20},{20,16},{24,28},{28,24},{1,5},{5... | collective-permute-start | bytes 29196296 | tf_op jit(solution)/shard_map/ppermute | solution.py:75
  498.8 48.7 %collective-permute-start.28 = (bf16[512,2048]{1,0:T(8,128)(2,1)}, bf16[512,2048]{1,0:T(8,128)(2,1)}, u32[]{:S(2)}, u32[]{:S(2)}) collective-permute-start(bf16[512,2048]{1,0:T(8,128)(2,1)} %get-tuple-element.158), channel_id=1, source_target_pairs={{0,8},{4,12},{8,0},{12,4},{16,24},{20,28},{24,16},{28,20},{1,9},{5... | collective-permute-start | bytes 6291464 | tf_op jit(solution)/shard_map/ppermute | solution.py:70
  499.3 93.0 %collective-permute-start.29 = (bf16[512,2048]{1,0:T(8,128)(2,1)}, bf16[512,2048]{1,0:T(8,128)(2,1)}, u32[]{:S(2)}, u32[]{:S(2)}) collective-permute-start(bf16[512,2048]{1,0:T(8,128)(2,1)} %get-tuple-element.159), channel_id=1, source_target_pairs={{0,16},{4,20},{8,24},{12,28},{16,0},{20,4},{24,8},{28,12},{1,17},{... | collective-permute-start | bytes 6291464 | tf_op jit(solution)/shard_map/ppermute | solution.py:70
  499.9 92.4 %collective-permute-start.30 = (bf16[512,2048]{1,0:T(8,128)(2,1)}, bf16[512,2048]{1,0:T(8,128)(2,1)}, u32[]{:S(2)}, u32[]{:S(2)}) collective-permute-start(bf16[512,2048]{1,0:T(8,128)(2,1)} %get-tuple-element.160), channel_id=1, source_target_pairs={{0,24},{4,28},{8,16},{12,20},{16,8},{20,12},{24,0},{28,4},{1,25},{... | collective-permute-start | bytes 6291464 | tf_op jit(solution)/shard_map/ppermute | solution.py:70
  502.3 267.2 %all-reduce.15.cloned.1.call-start = ((), (), s32[]{:S(2)}) async-start(), calls=%async_computation.4 | async-start | bytes 5505024 | tf_op jit(solution)/shard_map/psum | solution.py:964
  599.1 4.0 copy-start.6
  599.1 4.1 copy-start.8
  634.3 6.0 copy-start.13
  636.9 3.4 collective-permute-start.31
  643.5 16.8 %collective-permute-start.32 = (bf16[2,256,640]{2,1,0:T(8,128)(2,1)S(1)}, bf16[2,256,640]{2,1,0:T(8,128)(2,1)S(1)}, u32[]{:S(2)}, u32[]{:S(2)}) collective-permute-start(bf16[2,256,640]{2,1,0:T(8,128)(2,1)S(1)} %fusion.16), channel_id=1, source_target_pairs={{0,8},{4,12},{8,0},{12,4},{16,24},{20,28},{24,16},{28,20},{1,9},{5... | collective-permute-start | bytes 1966088 | tf_op jit(solution)/shard_map/ppermute | solution.py:70
  645.4 17.3 %copy-start.5 = (f32[512,512]{1,0:T(8,128)S(1)}, f32[512,512]{1,0:T(8,128)}, u32[]{:S(2)}) copy-start(f32[512,512]{1,0:T(8,128)} %get-tuple-element.178) | copy-start | bytes 3145732
  678.6 186.0 %all-to-all-start = ((bf16[4,4752,256]{2,1,0:T(8,128)(2,1)}), bf16[4,4752,256]{2,1,0:T(8,128)(2,1)}, u32[]{:S(2)}, u32[]{:S(2)}) async-start(bf16[4,4752,256]{2,1,0:T(8,128)(2,1)} %add_convert_fusion), calls=%async_computation | async-start | bytes 19464192 | tf_op jit(solution)/shard_map/all_to_all | solution.py:966
  684.5 86.1 %copy-start.16 = (f32[512,128]{1,0:T(8,128)S(1)}, f32[512,128]{1,0:T(8,128)}, u32[]{:S(2)}) copy-start(f32[512,128]{1,0:T(8,128)} %copy.74.sin_ref) | copy-start | bytes 786436
  684.5 86.1 %copy-start.17 = (f32[512,128]{1,0:T(8,128)S(1)}, f32[512,128]{1,0:T(8,128)}, u32[]{:S(2)}) copy-start(f32[512,128]{1,0:T(8,128)} %copy.73.cos_ref) | copy-start | bytes 786436
  684.5 203.0 %all-reduce.13.cloned.1.call-start = ((), (), s32[]{:S(2)}) async-start(), calls=%async_computation.3 | async-start | bytes 4194304 | tf_op jit(solution)/shard_map/psum | solution.py:972
  795.2 4.5 copy-start.14
  799.0 13.0 %collective-permute-start.38 = (bf16[4,1552,256]{2,1,0:T(8,128)(2,1)}, bf16[4,1552,256]{2,1,0:T(8,128)(2,1)}, u32[]{:S(2)}, u32[]{:S(2)}) collective-permute-start(bf16[4,1552,256]{2,1,0:T(8,128)(2,1)} %pad_maximum_fusion.1), channel_id=1, source_target_pairs={{0,4},{4,0},{8,12},{12,8},{16,20},{20,16},{24,28},{28,24},{1,5},{5... | collective-permute-start | bytes 9535496 | tf_op jit(solution)/shard_map/ppermute | solution.py:75
  801.3 5.4 collective-permute-start.34
  801.9 10.1 %copy-start.4 = (bf16[8,1280,256]{2,1,0:T(8,128)(2,1)S(1)}, bf16[8,1280,256]{2,1,0:T(8,128)(2,1)}, u32[]{:S(2)}) copy-start(bf16[8,1280,256]{2,1,0:T(8,128)(2,1)} %attend_grads.1) | copy-start | bytes 15728644
  808.4 10.1 %collective-permute-start.35 = (bf16[592,256]{1,0:T(8,128)(2,1)S(1)}, bf16[592,256]{1,0:T(8,128)(2,1)S(1)}, u32[]{:S(2)}, u32[]{:S(2)}) collective-permute-start(bf16[592,256]{1,0:T(8,128)(2,1)S(1)} %get-tuple-element.236), channel_id=1, source_target_pairs={{0,8},{4,12},{8,0},{12,4},{16,24},{20,28},{24,16},{28,20},{1,9},{5... | collective-permute-start | bytes 909320 | tf_op jit(solution)/shard_map/ppermute | solution.py:70
  810.0 16.0 %collective-permute-start.37 = (bf16[592,256]{1,0:T(8,128)(2,1)S(1)}, bf16[592,256]{1,0:T(8,128)(2,1)S(1)}, u32[]{:S(2)}, u32[]{:S(2)}) collective-permute-start(bf16[592,256]{1,0:T(8,128)(2,1)S(1)} %get-tuple-element.237), channel_id=1, source_target_pairs={{0,24},{4,28},{8,16},{12,20},{16,8},{20,12},{24,0},{28,4},{1,25},{... | collective-permute-start | bytes 909320 | tf_op jit(solution)/shard_map/ppermute | solution.py:70
  811.4 16.5 %collective-permute-start.36 = (bf16[592,256]{1,0:T(8,128)(2,1)S(1)}, bf16[592,256]{1,0:T(8,128)(2,1)S(1)}, u32[]{:S(2)}, u32[]{:S(2)}) collective-permute-start(bf16[592,256]{1,0:T(8,128)(2,1)S(1)} %get-tuple-element.238), channel_id=1, source_target_pairs={{0,16},{4,20},{8,24},{12,28},{16,0},{20,4},{24,8},{28,12},{1,17},{... | collective-permute-start | bytes 909320 | tf_op jit(solution)/shard_map/ppermute | solution.py:70
  814.5 27.6 %collective-permute-start.39 = (bf16[1552,256]{1,0:T(8,128)(2,1)S(1)}, bf16[1552,256]{1,0:T(8,128)(2,1)S(1)}, u32[]{:S(2)}, u32[]{:S(2)}) collective-permute-start(bf16[1552,256]{1,0:T(8,128)(2,1)S(1)} %get-tuple-element.227), channel_id=1, source_target_pairs={{0,8},{4,12},{8,0},{12,4},{16,24},{20,28},{24,16},{28,20},{1,9},{5... | collective-permute-start | bytes 2383880 | tf_op jit(solution)/shard_map/ppermute | solution.py:70
  816.0 43.3 %collective-permute-start.41 = (bf16[1552,256]{1,0:T(8,128)(2,1)S(1)}, bf16[1552,256]{1,0:T(8,128)(2,1)S(1)}, u32[]{:S(2)}, u32[]{:S(2)}) collective-permute-start(bf16[1552,256]{1,0:T(8,128)(2,1)S(1)} %get-tuple-element.228), channel_id=1, source_target_pairs={{0,24},{4,28},{8,16},{12,20},{16,8},{20,12},{24,0},{28,4},{1,25},{... | collective-permute-start | bytes 2383880 | tf_op jit(solution)/shard_map/ppermute | solution.py:70
  818.5 42.1 %collective-permute-start.40 = (bf16[1552,256]{1,0:T(8,128)(2,1)S(1)}, bf16[1552,256]{1,0:T(8,128)(2,1)S(1)}, u32[]{:S(2)}, u32[]{:S(2)}) collective-permute-start(bf16[1552,256]{1,0:T(8,128)(2,1)S(1)} %get-tuple-element.229), channel_id=1, source_target_pairs={{0,16},{4,20},{8,24},{12,28},{16,0},{20,4},{24,8},{28,12},{1,17},{... | collective-permute-start | bytes 2383880 | tf_op jit(solution)/shard_map/ppermute | solution.py:70
  871.9 15.7 %copy-start.1 = (bf16[2,256,2048]{2,1,0:T(8,128)(2,1)S(1)}, bf16[2,256,2048]{2,1,0:T(8,128)(2,1)}, u32[]{:S(2)}) copy-start(bf16[2,256,2048]{2,1,0:T(8,128)(2,1)} %param.18) | copy-start | bytes 6291460
  (6 other events, 12.5 us)
Sparse Core Ops, SparseCore 0:
  181.9 86.7 all-reduce.8
  502.4 83.6 all-reduce.10
  662.7 106.6 all-reduce.14
  802.0 85.4 all-reduce.12
